TPU v7x, 32 devices: a whole 2x2x4 slice. The times are simulated.
32 devices in a mesh: band: 4 (over y, core), slab: 8 (over z, x).
Axes of the slice: x: 2, y: 2, z: 4, core: 2. Of those that a mesh axis runs over, the one named last changes fastest.
Arguments:
- bands: float32 [2, 256, 32768], P(None, ('band', 'slab')), may hold values from -6 to 6
- projectors: float32 [4096, 512], P('slab'), may hold values from -0.625 to 0.625
- slot_atom: int32 [4096], P('slab'), may hold values from -1 to 767, as said below
- slot_box: int32 [4096], P('slab'), may hold values from 0 to 63
- channels: int32 [768], replicated, may hold values from 1 to 8
- coupling: float32 [8, 8, 768], replicated, may hold values from -2 to 2
Outputs:
- applied: float32 [2, 256, 32768], P(None, ('band', 'slab'))
Inputs may be any that keep to these rules, and one draw needn't show every extreme that they name: `slot_atom`: atom a is owned by slab a // 96. A live slot k names an atom owned by slab k // 512 or by the slab before it, cyclically. In each slab's 512 slots the live ones come first; some slab has all of its slots live.
All inputs are finite; a program needn't handle non-finite values.
Results may differ from a plain program's by a relative error of at most 0.0003.
Values sent between devices are 32-bit elements; how exact they have to be, the bound alone decides.
No kernel may reach another device: no remote copies, remote signals or barrier semaphores. Data moves between devices by JAX's collectives and lax.ppermute only.
A program may use at most 128 MiB of HBM per device.

v0:
```python
import collections
import functools
import math

import jax
import jax.numpy as jnp
import numpy as np
from jax import lax
from jax.experimental import pallas as pl
from jax.experimental.pallas import tpu as pltpu
from jax.sharding import PartitionSpec as P

BOXPTS = 64
GROUP = 16
INFO = 8
UNROLL = 4
AXES = ("band", "slab")
MIB = 1 << 20


def round_up(value, step):
    return (value + step - 1) // step * step


def cycle_tables(nslab):
    order = list(range(0, nslab, 2)) + list(range(nslab - 1 - nslab % 2, 0, -2))
    place = {s: i for i, s in enumerate(order)}
    return order, place


def params(limit):
    return pltpu.CompilerParams(vmem_limit_bytes=limit)


VMEM = pl.BlockSpec(memory_space=pltpu.VMEM)
SMEM = pl.BlockSpec(memory_space=pltpu.SMEM)
ANY = pl.BlockSpec(memory_space=pl.ANY)


def split_bands_kernel(x_ref, out_ref):
    rows = x_ref.shape[0]
    low_half = lax.broadcasted_iota(jnp.int32, (rows, 128), 1) < BOXPTS
    zero = jnp.zeros((rows, 128), jnp.float32)

    def step(pair, carry):
        x = x_ref[:, pl.ds(pl.multiple_of(pair * 128, 128), 128)]
        high = x.astype(jnp.bfloat16).astype(jnp.float32)
        low = x - high
        high_turned = pltpu.roll(high, BOXPTS, 1)
        low_turned = pltpu.roll(low, BOXPTS, 1)
        out_ref[2 * pair, :, 0:128] = jnp.where(low_half, high, high_turned).astype(jnp.bfloat16)
        out_ref[2 * pair, :, 128:256] = jnp.where(low_half, low, zero).astype(jnp.bfloat16)
        out_ref[2 * pair + 1, :, 0:128] = jnp.where(low_half, high_turned, high).astype(jnp.bfloat16)
        out_ref[2 * pair + 1, :, 128:256] = jnp.where(low_half, low_turned, zero).astype(jnp.bfloat16)
        return carry

    lax.fori_loop(0, x_ref.shape[1] // 128, step, 0, unroll=4)


def split_bands(x):
    rows, ngrid = x.shape
    shape = (ngrid // BOXPTS, rows, 256)
    return pl.pallas_call(
        split_bands_kernel,
        out_shape=jax.ShapeDtypeStruct(shape, jnp.bfloat16),
        in_specs=[VMEM],
        out_specs=VMEM,
        compiler_params=params(40 * MIB),
        cost_estimate=pl.CostEstimate(flops=8 * x.size, bytes_accessed=12 * x.size, transcendentals=0),
        name="split_bands",
    )(x)


def slot_weights(values, low_half, axis):
    full, top = [], []
    for t in range(values.shape[1] // 128):
        x = values[:, t * 128 : (t + 1) * 128]
        high = x.astype(jnp.bfloat16).astype(jnp.float32)
        low = x - high
        turned = pltpu.roll(high, BOXPTS, 1)
        full.append(jnp.where(low_half, high, pltpu.roll(low, BOXPTS, 1)).astype(jnp.bfloat16))
        full.append(jnp.where(low_half, turned, low).astype(jnp.bfloat16))
        top.append(jnp.where(low_half, high, 0.0).astype(jnp.bfloat16))
        top.append(jnp.where(low_half, turned, 0.0).astype(jnp.bfloat16))
    return jnp.concatenate(
        [jnp.concatenate(full, axis=0), jnp.concatenate(top, axis=0)], axis=axis
    )


def live_groups(live, start, length):
    return lax.div(jnp.clip(live - start, 0, length) + (GROUP - 1), GROUP)


def describe(slot_atom, slot_box, slab, nslab, natoms, width, lanes):
    atom_dev = natoms // nslab
    relative = (slot_atom - (slab + nslab - 1) % nslab * atom_dev) % natoms
    column = jnp.where(relative < atom_dev, relative, relative + (lanes - atom_dev))
    column = jnp.where(slot_atom >= 0, column, -1)
    live = jnp.broadcast_to(jnp.sum((slot_atom >= 0).astype(jnp.int32)), slot_atom.shape)
    rows = jnp.stack([slot_box, live, column]).astype(jnp.float32)
    return jnp.pad(rows, ((0, INFO - rows.shape[0]), (0, width - rows.shape[1])))


def project_kernel(pieces, infos, place_ref, x_ref, *refs):
    arrays = refs[: -len(pieces) - 3]
    outs = refs[-len(pieces) - 3 : -3]
    whole, table, sem = refs[-3:]
    copies = []
    for k, index in enumerate(infos):
        whole[k] = arrays[index][0:INFO, :].astype(jnp.int32)
        copies.append(pltpu.make_async_copy(whole.at[k], table.at[k], sem.at[k]))
        copies[-1].start()
    rows = x_ref.shape[1]
    width = outs[0].shape[2]
    low_half = lax.broadcasted_iota(jnp.int32, (GROUP, 128), 1) < BOXPTS
    lane_slot = lax.broadcasted_iota(jnp.int32, (rows, width), 1) % GROUP
    for out in outs:
        out[...] = jnp.zeros(out.shape, jnp.float32)
    for c in copies:
        c.wait()
    for p, out in zip(pieces, outs):
        array = arrays[p.array]
        start = place_ref[3 * p.index + 1]
        box_base = place_ref[3 * p.index + 2]
        info = infos.index(p.info)
        count = live_groups(table[info, 1, 0], start, p.rows)

        def step(block, carry):
            groups = [block * UNROLL + u for u in range(UNROLL)]
            weights, patches = [], []
            for g in groups:
                first = pl.multiple_of(p.offset + g * GROUP, 8)
                weights.append(slot_weights(array[pl.ds(first, GROUP), :], low_half, 1))
                boxes = [table[info, 0, start + g * GROUP + s] for s in range(GROUP)]
                patches.append(jnp.concatenate([x_ref[box_base + b] for b in boxes], axis=0))
            totals = []
            for w, p_ in zip(weights, patches):
                product = lax.dot_general(
                    p_, w, (((1,), (1,)), ((), ())), preferred_element_type=jnp.float32
                )
                total = product[0:rows]
                for s in range(1, GROUP):
                    total = jnp.where(lane_slot == s, product[s * rows : (s + 1) * rows], total)
                totals.append(total)
            for g, total in zip(groups, totals):
                out[g] = total
            return carry

        lax.fori_loop(0, lax.div(count + (UNROLL - 1), UNROLL), step, 0)


def project(arrays, pieces, place, x):
    channel = arrays[0].shape[1] // BOXPTS
    used = sorted({p.array for p in pieces} | {p.info for p in pieces})
    local = [
        p._replace(array=used.index(p.array), info=used.index(p.info)) for p in pieces
    ]
    infos = sorted({p.info for p in local})
    shapes = [
        jax.ShapeDtypeStruct((p.rows // GROUP, x.shape[1], channel * GROUP), jnp.float32)
        for p in pieces
    ]
    size = sum(p.rows for p in pieces) * arrays[0].shape[1]
    table = (len(infos), INFO, arrays[0].shape[1])
    return pl.pallas_call(
        functools.partial(project_kernel, local, infos),
        out_shape=shapes,
        in_specs=[SMEM, VMEM] + [VMEM] * len(used),
        out_specs=[VMEM] * len(pieces),
        scratch_shapes=[
            pltpu.VMEM(table, jnp.int32),
            pltpu.SMEM(table, jnp.int32),
            pltpu.SemaphoreType.DMA((len(infos),)),
        ],
        compiler_params=params(40 * MIB),
        cost_estimate=pl.CostEstimate(
            flops=2 * 16 * 16 * size, bytes_accessed=4 * size + 2 * x.size, transcendentals=0
        ),
        name="project",
    )(place, x, *[arrays[i] for i in used])


def swap_blocks(tiles, lane_block, width):
    tiles = list(tiles)
    bit = 1
    while bit < len(tiles):
        upper = (lane_block & bit) != 0
        for i in range(len(tiles)):
            if not i & bit:
                a, b = tiles[i], tiles[i | bit]
                tiles[i] = jnp.where(upper, pltpu.roll(b, GROUP * bit, 1), a)
                tiles[i | bit] = jnp.where(upper, b, pltpu.roll(a, width - GROUP * bit, 1))
        bit *= 2
    return tiles


def stacked_split(value):
    high = value.astype(jnp.bfloat16)
    low = (value - high.astype(jnp.float32)).astype(jnp.bfloat16)
    return jnp.concatenate([high, low], axis=0)


def apply_kernel(nslab, slots, pieces, infos, place_ref, coupling_ref, *refs):
    npiece = len(pieces)
    proj, parts, beta, sums, done, masks, info, whole, table = refs[-13:-4]
    beta_sem, proj_sem, info_sem, out_sem = refs[-4:]
    out_ref = refs[-14]
    projections = refs[-14 - npiece : -14]
    arrays = refs[: -14 - npiece]
    groups = slots // GROUP
    rows, width = proj.shape[1], proj.shape[2]
    channel = width // GROUP
    lanes = parts.shape[2] // 2
    boxes = out_ref.shape[1] // BOXPTS // nslab
    chunk = width // GROUP
    info_copies, copies, beta_copies = [], [], []
    for i, (array, index) in enumerate(infos):
        slab = place_ref[3 * index]
        info_copies.append(
            pltpu.make_async_copy(arrays[array].at[0:INFO, :], info.at[slab], info_sem.at[i])
        )
    for i, p in enumerate(pieces):
        slab, start = place_ref[3 * p.index], place_ref[3 * p.index + 1]
        first = slab * groups + lax.div(start, GROUP)
        copies.append(
            pltpu.make_async_copy(
                projections[i], proj.at[pl.ds(first, p.rows // GROUP)], proj_sem.at[i]
            )
        )
        first = pl.multiple_of(slab * slots + start, GROUP)
        beta_copies.append(
            pltpu.make_async_copy(
                arrays[p.array].at[p.offset : p.offset + p.rows, :],
                beta.at[pl.ds(first, p.rows), :],
                beta_sem.at[i],
            )
        )
    for c in info_copies + copies + beta_copies:
        c.start()
    lane_slot = lax.broadcasted_iota(jnp.int32, (rows, width), 1) % GROUP
    for s in range(GROUP):
        masks[s] = jnp.where(lane_slot == s, 1.0, 0.0).astype(jnp.bfloat16)
    for c in info_copies:
        c.wait()
    whole[...] = info[...].astype(jnp.int32)
    to_scalars = pltpu.make_async_copy(whole, table, info_sem.at[0])
    to_scalars.start()
    for j in range(sums.shape[0]):
        sums[j] = jnp.zeros(sums.shape[1:], jnp.float32)
    parts[...] = jnp.zeros(parts.shape, jnp.float32)
    to_scalars.wait()
    for c in copies:
        c.wait()

    lane_block = lax.broadcasted_iota(jnp.int32, (rows, width), 1) // GROUP
    atom_row = lax.broadcasted_iota(jnp.int32, (2 * lanes, width), 0).astype(jnp.float32)

    def selector(slab, k):
        first = pl.multiple_of(k * width, 128)
        column = jnp.broadcast_to(info[slab, 2:3, pl.ds(first, width)], (2 * lanes, width))
        return jnp.where(column == atom_row, 1.0, 0.0).astype(jnp.bfloat16)

    def chunks(slab):
        return lax.div(table[slab, 1, 0] + (width - 1), width)

    def sum_by_atom(slab, carry):
        def step(k, inner):
            first = slab * groups + k * chunk
            tiles = [proj[first + i] for i in range(chunk)]
            value = jnp.concatenate(swap_blocks(tiles, lane_block, width), axis=0)
            both = lax.dot_general(
                stacked_split(value),
                selector(slab, k),
                (((1,), (1,)), ((), ())),
                preferred_element_type=jnp.float32,
            )
            half = both.shape[0] // 2
            parts[slab] = parts[slab] + (both[:half] + both[half:])
            return inner

        lax.fori_loop(0, chunks(slab), step, 0)
        return carry

    lax.fori_loop(0, nslab, sum_by_atom, 0)

    def couple(slab, carry):
        following = lax.rem(slab + 1, nslab)
        total = parts[slab, :, lanes:] + parts[following, :, :lanes]
        for c in range(channel):
            mixed = jnp.zeros((rows, lanes), jnp.float32)
            for e in range(channel):
                factor = coupling_ref[slab, pl.ds(c * channel + e, 1), :]
                mixed = mixed + factor * total[e * rows : (e + 1) * rows]
            parts[slab, c * rows : (c + 1) * rows, lanes:] = mixed
        return carry

    lax.fori_loop(0, nslab, couple, 0)

    def spread(slab, carry):
        below = lax.rem(slab + nslab - 1, nslab)
        value = jnp.concatenate([parts[below, :, lanes:], parts[slab, :, lanes:]], axis=1)
        value = stacked_split(value)

        def step(k, inner):
            both = jnp.dot(value, selector(slab, k), preferred_element_type=jnp.float32)
            half = both.shape[0] // 2
            both = both[:half] + both[half:]
            tiles = [both[c * rows : (c + 1) * rows] for c in range(channel)]
            for i, tile in enumerate(swap_blocks(tiles, lane_block, width)):
                proj[slab * groups + k * chunk + i] = tile
            return inner

        lax.fori_loop(0, chunks(slab), step, 0)
        return carry

    lax.fori_loop(0, nslab, spread, 0)

    nsum = sums.shape[0]
    for c in beta_copies:
        c.wait()

    low_half = lax.broadcasted_iota(jnp.int32, (GROUP, 128), 1) < BOXPTS
    pair_half = lax.broadcasted_iota(jnp.int32, (rows, 128), 1) < BOXPTS
    span = boxes * BOXPTS

    def leaving(slab):
        slot = lax.rem(slab, 2)
        return pltpu.make_async_copy(
            done.at[slot],
            out_ref.at[:, pl.ds(pl.multiple_of(slab * span, 128), span)],
            out_sem.at[slot],
        )

    def slab_step(slab, carry):
        def step(block, inner):
            products = []
            for u in range(UNROLL):
                g = block * UNROLL + u
                slot_base = pl.multiple_of(slab * slots + g * GROUP, GROUP)
                weights = slot_weights(beta[pl.ds(slot_base, GROUP), :], low_half, 0)
                c = proj[slab * groups + g]
                high = c.astype(jnp.bfloat16)
                low = (c - high.astype(jnp.float32)).astype(jnp.bfloat16)
                left = jnp.concatenate(
                    [
                        jnp.concatenate([high * masks[s], low * masks[s]], axis=1)
                        for s in range(GROUP)
                    ],
                    axis=0,
                )
                products.append((slot_base, jnp.dot(left, weights, preferred_element_type=jnp.float32)))
            for u, (slot_base, product) in enumerate(products):
                for s in range(GROUP):
                    box = slab * boxes + table[slab, 0, block * (UNROLL * GROUP) + u * GROUP + s]
                    j = (u * GROUP + s) % nsum
                    sums[j, box] = sums[j, box] + product[s * rows : (s + 1) * rows]
            return inner

        count = live_groups(table[slab, 1, 0], 0, slots)
        lax.fori_loop(0, lax.div(count + (UNROLL - 1), UNROLL), step, 0)

        @pl.when(slab >= 2)
        def _():
            leaving(slab - 2).wait()

        def finish(pair, inner):
            folded = []
            for i in range(2):
                box = slab * boxes + 2 * pair + i
                value = sums[0, box]
                for j in range(1, nsum):
                    value = value + sums[j, box]
                folded.append(value + pltpu.roll(value, BOXPTS, 1))
            done[lax.rem(slab, 2), :, pl.ds(pl.multiple_of(pair * 128, 128), 128)] = jnp.where(
                pair_half, folded[0], folded[1]
            )
            return inner

        lax.fori_loop(0, span // 128, finish, 0, unroll=8)
        leaving(slab).start()
        return carry

    lax.fori_loop(0, nslab, slab_step, 0)
    for slab in range(max(nslab - 2, 0), nslab):
        leaving(slab).wait()


def apply(arrays, pieces, infos, projections, place, coupling, nslab, slots, rows, ngrid):
    width = projections[0].shape[2]
    lanes = coupling.shape[2]
    depth = arrays[0].shape[1]
    one_sum = ngrid // BOXPTS * rows * 128 * 4
    nsum = 2 if one_sum <= 8 * MIB else 1
    buffers = [
        pltpu.VMEM((nslab * slots // GROUP, rows, width), jnp.float32),
        pltpu.VMEM((nslab, width // GROUP * rows, 2 * lanes), jnp.float32),
        pltpu.VMEM((nslab * slots, depth), jnp.float32),
        pltpu.VMEM((nsum, ngrid // BOXPTS, rows, 128), jnp.float32),
        pltpu.VMEM((2, rows, ngrid // nslab), jnp.float32),
        pltpu.VMEM((GROUP, rows, width), jnp.bfloat16),
        pltpu.VMEM((nslab, INFO, depth), jnp.float32),
        pltpu.VMEM((nslab, INFO, depth), jnp.int32),
    ]
    need = sum(math.prod(b.shape) * b.dtype.itemsize for b in buffers)
    scratch = buffers + [
        pltpu.SMEM((nslab, INFO, depth), jnp.int32),
        pltpu.SemaphoreType.DMA((len(pieces),)),
        pltpu.SemaphoreType.DMA((len(pieces),)),
        pltpu.SemaphoreType.DMA((len(infos),)),
        pltpu.SemaphoreType.DMA((2,)),
    ]
    return pl.pallas_call(
        functools.partial(apply_kernel, nslab, slots, pieces, infos),
        out_shape=jax.ShapeDtypeStruct((rows, ngrid), jnp.float32),
        in_specs=[SMEM, VMEM] + [ANY] * (len(arrays) + len(pieces)),
        out_specs=ANY,
        scratch_shapes=scratch,
        compiler_params=params(min(need + 4 * MIB, 63 * MIB)),
        name="apply",
    )(place, coupling, *arrays, *projections)


Piece = collections.namedtuple("Piece", ["array", "offset", "rows", "info", "index"])


def gather_pieces(projectors, described, nband, nslab):
    slots = projectors.shape[0]
    order, at = cycle_tables(nslab)
    half = slots // 2
    quarter = half // 2
    reach = nslab // 2
    onward = [
        (b * nslab + order[i], b * nslab + order[(i + 1) % nslab])
        for b in range(nband)
        for i in range(nslab)
    ]
    backward = [(d, s) for s, d in onward]
    sibling = [(b * nslab + s, (b ^ 1) * nslab + s) for b in range(nband) for s in range(nslab)]
    core = lax.rem(lax.axis_index("band"), 2)
    mine = lax.dynamic_slice_in_dim(projectors, core * half, half, 0)
    mine = jnp.concatenate([described, mine], axis=0)
    arrays, pieces, calls, infos = [described, projectors], [Piece(1, 0, slots, 0, 0)], [[0]], [(0, 0)]
    places = [lambda core, slab: (slab, 0)]

    def add(array, distance, start, other, info=None):
        arrays.append(array)
        own = len(arrays) - 1
        offset = INFO if info is None else 0
        info = own if info is None else info
        pieces.append(Piece(own, offset, array.shape[0] - offset, info, len(places)))
        places.append(
            lambda core, slab: (
                order[(at[slab] + distance) % nslab],
                (1 - core if other else core) * half + start,
            )
        )
        return len(pieces) - 1

    waiting = []
    up = down = mine
    for step in range(1, reach):
        up = lax.ppermute(up, AXES, onward)
        down = lax.ppermute(down, AXES, backward)
        now = [add(up, -step, 0, False), add(down, step, 0, False)]
        infos += [(pieces[i].array, pieces[i].index) for i in now]
        calls.append(now + waiting)
        waiting = [
            add(lax.ppermute(up, AXES, sibling), -step, 0, True),
            add(lax.ppermute(down, AXES, sibling), step, 0, True),
        ]
    up = lax.ppermute(up[: INFO + quarter], AXES, onward)
    down = lax.ppermute(down[INFO + quarter :], AXES, backward)
    first = add(up, reach, 0, False)
    infos.append((pieces[first].array, pieces[first].index))
    calls.append([first, add(down, reach, quarter, False, pieces[first].array)] + waiting)
    first = add(lax.ppermute(up, AXES, sibling), reach, 0, True)
    second = add(
        lax.ppermute(down, AXES, sibling), reach, quarter, True, pieces[first].array
    )
    calls.append([first, second])
    return arrays, pieces, calls, infos, places


def body(bands, projectors, slot_atom, slot_box, channels, coupling):
    nblock, band_local, ngrid = bands.shape
    nband, nslab = lax.axis_size("band"), lax.axis_size("slab")
    natoms = channels.shape[0]
    atom_dev = natoms // nslab
    channel = coupling.shape[0]
    slots = slot_atom.shape[0]
    lanes = round_up(atom_dev, 128)

    slab = lax.axis_index("slab")
    described = describe(slot_atom, slot_box, slab, nslab, natoms, projectors.shape[1], lanes)
    arrays, pieces, calls, infos, places = gather_pieces(projectors, described, nband, nslab)
    table = np.array(
        [[p(b % 2, s) for p in places] for b in range(nband) for s in range(nslab)], np.int32
    )
    boxes = ngrid // BOXPTS // nslab
    table = np.concatenate([table, table[:, :, :1] * boxes], axis=2)
    me = lax.axis_index("band") * nslab + slab
    place = lax.dynamic_index_in_dim(jnp.asarray(table), me, 0, keepdims=False).reshape(-1)

    mask = (jnp.arange(channel, dtype=jnp.int32)[:, None] < channels[None, :]).astype(jnp.float32)
    masked = coupling * mask[:, None, :] * mask[None, :, :]
    masked = masked.reshape(channel * channel, nslab, atom_dev).transpose(1, 0, 2)
    masked = jnp.pad(masked, ((0, 0), (0, 0), (0, lanes - atom_dev)))

    rows = nblock * band_local
    padded = round_up(rows, GROUP)
    x = bands.reshape(rows, ngrid)
    if padded != rows:
        x = jnp.pad(x, ((0, padded - rows), (0, 0)))
    split = split_bands(x)
    projections = [None] * len(pieces)
    for call in calls:
        for i, value in zip(call, project(arrays, [pieces[i] for i in call], place, split)):
            projections[i] = value
    out = apply(arrays, pieces, infos, projections, place, masked, nslab, slots, padded, ngrid)
    return out[:rows].reshape(nblock, band_local, ngrid)


def solution(mesh):
    in_specs = (P(None, ("band", "slab"), None), P("slab", None), P("slab"), P("slab"), P(), P())
    out_specs = P(None, ("band", "slab"), None)
    return jax.shard_map(body, mesh=mesh, in_specs=in_specs, out_specs=out_specs, check_vma=False)
```

profile of v0, /device:TPU:1, one launch (start us, length us, event | category | flops | bytes accessed | tf_op | source)
XLA Modules:
  0.0 136.7 jit_solution(6101238158656899979)
XLA Ops:
  0.0 1.3 convert_reduce_fusion
  2.8 1.1 constant_dynamic-slice_fusion
  3.9 2.2 %collective-permute-start = (f32[264,512]{1,0:T(8,128)S(1)}, f32[264,512]{1,0:T(8,128)}, u32[]{:S(2)}, u32[]{:S(2)}) collective-permute-start(f32[264,512]{1,0:T(8,128)S(1)} %pad_maximum_fusion), channel_id=1, source_target_pairs={{0,2},{2,4},{4,6},{6,7},{7,5},{5,3},{3,1},{1,0},{8,10},{10,12},{12... | collective-permute-start | bytes 1622024 | tf_op jit(solution)/shard_map/ppermute | solution.py:462
  6.1 12.0 %collective-permute-done.refs_0_.refs_2_ = f32[264,512]{1,0:T(8,128)} collective-permute-done((f32[264,512]{1,0:T(8,128)S(1)}, f32[264,512]{1,0:T(8,128)}, u32[]{:S(2)}, u32[]{:S(2)}) %collective-permute-start) | collective-permute-done | bytes 540704 | tf_op jit(solution)/shard_map/ppermute | solution.py:462
  18.1 1.2 collective-permute-start.4
  19.6 11.3 %collective-permute-done.4.refs_2_.refs_6_ = f32[264,512]{1,0:T(8,128)S(1)} collective-permute-done((f32[264,512]{1,0:T(8,128)}, f32[264,512]{1,0:T(8,128)S(1)}, u32[]{:S(2)}, u32[]{:S(2)}) %collective-permute-start.4) | collective-permute-done | bytes 540704 | tf_op jit(solution)/shard_map/ppermute | solution.py:462
  32.4 2.7 %collective-permute-start.2 = (f32[264,512]{1,0:T(8,128)}, f32[264,512]{1,0:T(8,128)S(1)}, u32[]{:S(2)}, u32[]{:S(2)}) collective-permute-start(f32[264,512]{1,0:T(8,128)} %collective-permute-done.refs_0_.refs_2_), channel_id=1, source_target_pairs={{0,8},{1,9},{2,10},{3,11},{4,12},{5,13},{6,14},{7,15},{8,0},{9,1},... | collective-permute-start | bytes 1622024 | tf_op jit(solution)/shard_map/ppermute | solution.py:468
  35.6 6.9 %collective-permute-done.8.refs_2_.refs_10_ = f32[264,512]{1,0:T(8,128)S(1)} collective-permute-done((f32[264,512]{1,0:T(8,128)S(1)}, f32[264,512]{1,0:T(8,128)S(1)}, u32[]{:S(2)}, u32[]{:S(2)}) %collective-permute-start.8) | collective-permute-done | bytes 540704 | tf_op jit(solution)/shard_map/ppermute | solution.py:462
  42.5 3.1 %collective-permute-start.7 = (f32[264,512]{1,0:T(8,128)S(1)}, f32[264,512]{1,0:T(8,128)}, u32[]{:S(2)}, u32[]{:S(2)}) collective-permute-start(f32[264,512]{1,0:T(8,128)S(1)} %collective-permute-done.5.refs_3_.refs_7_), channel_id=1, source_target_pairs={{0,8},{1,9},{2,10},{3,11},{4,12},{5,13},{6,14},{7,15},{8,0},{9,1},... | collective-permute-start | bytes 1622024 | tf_op jit(solution)/shard_map/ppermute | solution.py:469
  46.3 0.9 collective-permute-start.12
  50.8 4.4 %collective-permute-done.13.refs_3_.refs_15_ = f32[128,512]{1,0:T(8,128)} collective-permute-done((f32[128,512]{1,0:T(8,128)}, f32[128,512]{1,0:T(8,128)}, u32[]{:S(2)}, u32[]{:S(2)}) %collective-permute-start.13) | collective-permute-done | bytes 262176 | tf_op jit(solution)/shard_map/ppermute | solution.py:472
  55.2 1.7 %collective-permute-start.15 = (f32[128,512]{1,0:T(8,128)}, f32[128,512]{1,0:T(8,128)}, u32[]{:S(2)}, u32[]{:S(2)}) collective-permute-start(f32[128,512]{1,0:T(8,128)} %collective-permute-done.13.refs_3_.refs_15_), channel_id=1, source_target_pairs={{0,8},{1,9},{2,10},{3,11},{4,12},{5,13},{6,14},{7,15},{8,0},{9,1},... | collective-permute-start | bytes 786440 | tf_op jit(solution)/shard_map/ppermute | solution.py:478
  57.0 1.6 %multiply_multiply_fusion = f32[8,8,768]{2,1,0:T(8,128)} fusion(f32[8,8,768]{2,1,0:T(8,128)} %param.12, f32[8,768]{1,0:T(8,128)S(1)} %fusion), kind=kLoop, calls=%fused_computation.2 | loop fusion | flops 98304 | bytes 417792 | tf_op jit(solution)/shard_map/mul | solution.py:505
  58.6 1.8 %reshape.52 = f32[64,8,96]{2,1,0:T(8,128)} reshape(f32[8,8,768]{2,1,0:T(8,128)} %multiply_multiply_fusion) | data formatting | bytes 393216 | tf_op jit(solution)/shard_map/reshape | solution.py:506
  60.4 1.0 copy.10
  61.4 1.6 %copy-done.1 = f32[2,8,32768]{2,1,0:T(8,128)S(1)} copy-done((f32[2,8,32768]{2,1,0:T(8,128)S(1)}, f32[2,8,32768]{2,1,0:T(8,128)}, u32[]{:S(2)}) %copy-start.1) | copy-done | bytes 2097176
  63.0 5.4 %split_bands.1.x_ref = bf16[512,16,256]{2,1,0:T(8,128)(2,1)S(1)} custom-call(f32[16,32768]{1,0:T(8,128)S(1)} %bitcast.8), custom_call_target="tpu_custom_call" | custom-call | flops 4194304 | bytes 6291456 | tf_op jit(solution)/shard_map/split_bands/pallas_call | solution.py:63
  68.4 2.5 %project.6.refs_18_ = f32[32,16,128]{2,1,0:T(8,128)S(1)} custom-call(s32[51]{0:T(128)S(1)} %reshape.51.place_ref, bf16[512,16,256]{2,1,0:T(8,128)(2,1)S(1)} %split_bands.1.x_ref, f32[8,512]{1,0:T(8,128)S(1)} %pad.9.refs_0_, f32[512,512]{1,0:T(8,128)S(1)} %copy-done), custom_call_target="tpu_custom_call" | custom-call | flops 134217728 | bytes 5242880 | tf_op jit(solution)/shard_map/project/pallas_call | solution.py:165
  70.9 3.9 %project.7 = (f32[16,16,128]{2,1,0:T(8,128)S(1)}, f32[16,16,128]{2,1,0:T(8,128)S(1)}) custom-call(s32[51]{0:T(128)S(1)} %reshape.51.place_ref, bf16[512,16,256]{2,1,0:T(8,128)(2,1)S(1)} %split_bands.1.x_ref, f32[264,512]{1,0:T(8,128)} %collective-permute-done.refs_0_.refs_2_, f32[264,512]{1,0:T(8,128)} %collective-permute-done.1.refs_1_.refs_3_), custom_call_target="tpu_custom_call" | custom-call | flops 134217728 | bytes 5242880 | tf_op jit(solution)/shard_map/project/pallas_call | solution.py:165
  74.8 5.3 %project.8 = (f32[16,16,128]{2,1,0:T(8,128)S(1)}, f32[16,16,128]{2,1,0:T(8,128)S(1)}, f32[16,16,128]{2,1,0:T(8,128)S(1)}, f32[16,16,128]{2,1,0:T(8,128)S(1)}) custom-call(s32[51]{0:T(128)S(1)} %reshape.51.place_ref, bf16[512,16,256]{2,1,0:T(8,128)(2,1)S(1)} %split_bands.1.x_ref, f32[264,512]{1,0:T(8,128)S(1)} %collective-permute-done.2.refs_0_.refs_4_, ...), custom_call_target="tpu_custom_call" | custom-call | flops 268435456 | bytes 6291456 | tf_op jit(solution)/shard_map/project/pallas_call | solution.py:165
  80.1 6.7 %project.9 = (f32[16,16,128]{2,1,0:T(8,128)S(1)}, f32[16,16,128]{2,1,0:T(8,128)S(1)}, f32[16,16,128]{2,1,0:T(8,128)S(1)}, f32[16,16,128]{2,1,0:T(8,128)S(1)}) custom-call(s32[51]{0:T(128)S(1)} %reshape.51.place_ref, bf16[512,16,256]{2,1,0:T(8,128)(2,1)S(1)} %split_bands.1.x_ref, f32[264,512]{1,0:T(8,128)} %collective-permute-done.6.refs_0_.refs_8_, ...), custom_call_target="tpu_custom_call" | custom-call | flops 268435456 | bytes 6291456 | tf_op jit(solution)/shard_map/project/pallas_call | solution.py:165
  86.9 4.6 %project.10 = (f32[8,16,128]{2,1,0:T(8,128)S(1)}, f32[8,16,128]{2,1,0:T(8,128)S(1)}, f32[16,16,128]{2,1,0:T(8,128)S(1)}, f32[16,16,128]{2,1,0:T(8,128)S(1)}) custom-call(s32[51]{0:T(128)S(1)} %reshape.51.place_ref, bf16[512,16,256]{2,1,0:T(8,128)(2,1)S(1)} %split_bands.1.x_ref, f32[264,512]{1,0:T(8,128)} %collective-permute-done.10.refs_0_.refs_12_, ...), custom_call_target="tpu_custom_call" | custom-call | flops 201326592 | bytes 5767168 | tf_op jit(solution)/shard_map/project/pallas_call | solution.py:165
  91.5 2.6 %project.11 = (f32[8,16,128]{2,1,0:T(8,128)S(1)}, f32[8,16,128]{2,1,0:T(8,128)S(1)}) custom-call(s32[51]{0:T(128)S(1)} %reshape.51.place_ref, bf16[512,16,256]{2,1,0:T(8,128)(2,1)S(1)} %split_bands.1.x_ref, f32[136,512]{1,0:T(8,128)} %collective-permute-done.14.refs_0_.refs_16_, f32[128,512]{1,0:T(8,128)} %collective-permute-done.15.refs_1_.refs_17_), custom_call_target="tpu_custom_call" | custom-call | flops 67108864 | bytes 4718592 | tf_op jit(solution)/shard_map/project/pallas_call | solution.py:165
  94.2 42.5 %apply.1 = f32[16,32768]{1,0:T(8,128)} custom-call(s32[51]{0:T(128)S(1)} %reshape.51.place_ref, f32[8,64,128]{2,1,0:T(8,128)S(1)} %pad.8.coupling_ref, f32[8,512]{1,0:T(8,128)S(1)} %pad.9.refs_0_, f32[512,512]{1,0:T(8,128)S(1)} %copy-done, f32[264,512]{1,0:T(8,128)} %collective-permute-done.refs_0_.refs_2_, ...), custom_call_target="tpu_custom_call" | custom-call | tf_op jit(solution)/shard_map/apply/pallas_call | solution.py:412
  (35 shorter events, 8.1 us)
Async XLA Ops:
  3.9 14.2 %collective-permute-start = (f32[264,512]{1,0:T(8,128)S(1)}, f32[264,512]{1,0:T(8,128)}, u32[]{:S(2)}, u32[]{:S(2)}) collective-permute-start(f32[264,512]{1,0:T(8,128)S(1)} %pad_maximum_fusion), channel_id=1, source_target_pairs={{0,2},{2,4},{4,6},{6,7},{7,5},{5,3},{3,1},{1,0},{8,10},{10,12},{12... | collective-permute-start | bytes 1622024 | tf_op jit(solution)/shard_map/ppermute | solution.py:462
  6.1 13.3 %collective-permute-start.1 = (f32[264,512]{1,0:T(8,128)S(1)}, f32[264,512]{1,0:T(8,128)}, u32[]{:S(2)}, u32[]{:S(2)}) collective-permute-start(f32[264,512]{1,0:T(8,128)S(1)} %pad_maximum_fusion), channel_id=1, source_target_pairs={{2,0},{4,2},{6,4},{7,6},{5,7},{3,5},{1,3},{0,1},{10,8},{12,10},{14... | collective-permute-start | bytes 1622024 | tf_op jit(solution)/shard_map/ppermute | solution.py:463
  18.1 12.8 %collective-permute-start.4 = (f32[264,512]{1,0:T(8,128)}, f32[264,512]{1,0:T(8,128)S(1)}, u32[]{:S(2)}, u32[]{:S(2)}) collective-permute-start(f32[264,512]{1,0:T(8,128)} %collective-permute-done.refs_0_.refs_2_), channel_id=1, source_target_pairs={{0,2},{2,4},{4,6},{6,7},{7,5},{5,3},{3,1},{1,0},{8,10},{10,12},{12... | collective-permute-start | bytes 1622024 | tf_op jit(solution)/shard_map/ppermute | solution.py:462
  19.4 12.4 %collective-permute-start.5 = (f32[264,512]{1,0:T(8,128)}, f32[264,512]{1,0:T(8,128)S(1)}, u32[]{:S(2)}, u32[]{:S(2)}) collective-permute-start(f32[264,512]{1,0:T(8,128)} %collective-permute-done.1.refs_1_.refs_3_), channel_id=1, source_target_pairs={{2,0},{4,2},{6,4},{7,6},{5,7},{3,5},{1,3},{0,1},{10,8},{12,10},{14... | collective-permute-start | bytes 1622024 | tf_op jit(solution)/shard_map/ppermute | solution.py:463
  30.9 11.6 %collective-permute-start.8 = (f32[264,512]{1,0:T(8,128)S(1)}, f32[264,512]{1,0:T(8,128)S(1)}, u32[]{:S(2)}, u32[]{:S(2)}) collective-permute-start(f32[264,512]{1,0:T(8,128)S(1)} %collective-permute-done.4.refs_2_.refs_6_), channel_id=1, source_target_pairs={{0,2},{2,4},{4,6},{6,7},{7,5},{5,3},{3,1},{1,0},{8,10},{10,12},{12... | collective-permute-start | bytes 1622024 | tf_op jit(solution)/shard_map/ppermute | solution.py:462
  31.8 14.5 %collective-permute-start.9 = (f32[264,512]{1,0:T(8,128)S(1)}, f32[264,512]{1,0:T(8,128)S(1)}, u32[]{:S(2)}, u32[]{:S(2)}) collective-permute-start(f32[264,512]{1,0:T(8,128)S(1)} %collective-permute-done.5.refs_3_.refs_7_), channel_id=1, source_target_pairs={{2,0},{4,2},{6,4},{7,6},{5,7},{3,5},{1,3},{0,1},{10,8},{12,10},{14... | collective-permute-start | bytes 1622024 | tf_op jit(solution)/shard_map/ppermute | solution.py:463
  32.4 15.6 %collective-permute-start.2 = (f32[264,512]{1,0:T(8,128)}, f32[264,512]{1,0:T(8,128)S(1)}, u32[]{:S(2)}, u32[]{:S(2)}) collective-permute-start(f32[264,512]{1,0:T(8,128)} %collective-permute-done.refs_0_.refs_2_), channel_id=1, source_target_pairs={{0,8},{1,9},{2,10},{3,11},{4,12},{5,13},{6,14},{7,15},{8,0},{9,1},... | collective-permute-start | bytes 1622024 | tf_op jit(solution)/shard_map/ppermute | solution.py:468
  35.1 13.5 %collective-permute-start.3 = (f32[264,512]{1,0:T(8,128)}, f32[264,512]{1,0:T(8,128)S(1)}, u32[]{:S(2)}, u32[]{:S(2)}) collective-permute-start(f32[264,512]{1,0:T(8,128)} %collective-permute-done.1.refs_1_.refs_3_), channel_id=1, source_target_pairs={{0,8},{1,9},{2,10},{3,11},{4,12},{5,13},{6,14},{7,15},{8,0},{9,1},... | collective-permute-start | bytes 1622024 | tf_op jit(solution)/shard_map/ppermute | solution.py:469
  35.1 14.2 %collective-permute-start.6 = (f32[264,512]{1,0:T(8,128)S(1)}, f32[264,512]{1,0:T(8,128)}, u32[]{:S(2)}, u32[]{:S(2)}) collective-permute-start(f32[264,512]{1,0:T(8,128)S(1)} %collective-permute-done.4.refs_2_.refs_6_), channel_id=1, source_target_pairs={{0,8},{1,9},{2,10},{3,11},{4,12},{5,13},{6,14},{7,15},{8,0},{9,1},... | collective-permute-start | bytes 1622024 | tf_op jit(solution)/shard_map/ppermute | solution.py:468
  42.5 37.6 %collective-permute-start.7 = (f32[264,512]{1,0:T(8,128)S(1)}, f32[264,512]{1,0:T(8,128)}, u32[]{:S(2)}, u32[]{:S(2)}) collective-permute-start(f32[264,512]{1,0:T(8,128)S(1)} %collective-permute-done.5.refs_3_.refs_7_), channel_id=1, source_target_pairs={{0,8},{1,9},{2,10},{3,11},{4,12},{5,13},{6,14},{7,15},{8,0},{9,1},... | collective-permute-start | bytes 1622024 | tf_op jit(solution)/shard_map/ppermute | solution.py:469
  46.3 10.7 %collective-permute-start.12 = (f32[136,512]{1,0:T(8,128)}, f32[136,512]{1,0:T(8,128)S(1)}, u32[]{:S(2)}, u32[]{:S(2)}) collective-permute-start(f32[136,512]{1,0:T(8,128)} %slice.8), channel_id=1, source_target_pairs={{0,2},{2,4},{4,6},{6,7},{7,5},{5,3},{3,1},{1,0},{8,10},{10,12},{12... | collective-permute-start | bytes 835592 | tf_op jit(solution)/shard_map/ppermute | solution.py:471
  48.0 7.3 %collective-permute-start.13 = (f32[128,512]{1,0:T(8,128)}, f32[128,512]{1,0:T(8,128)}, u32[]{:S(2)}, u32[]{:S(2)}) collective-permute-start(f32[128,512]{1,0:T(8,128)} %slice.9), channel_id=1, source_target_pairs={{2,0},{4,2},{6,4},{7,6},{5,7},{3,5},{1,3},{0,1},{10,8},{12,10},{14... | collective-permute-start | bytes 786440 | tf_op jit(solution)/shard_map/ppermute | solution.py:472
  48.5 38.3 %collective-permute-start.10 = (f32[264,512]{1,0:T(8,128)S(1)}, f32[264,512]{1,0:T(8,128)}, u32[]{:S(2)}, u32[]{:S(2)}) collective-permute-start(f32[264,512]{1,0:T(8,128)S(1)} %collective-permute-done.8.refs_2_.refs_10_), channel_id=1, source_target_pairs={{0,8},{1,9},{2,10},{3,11},{4,12},{5,13},{6,14},{7,15},{8,0},{9,1},... | collective-permute-start | bytes 1622024 | tf_op jit(solution)/shard_map/ppermute | solution.py:468
  49.3 37.6 %collective-permute-start.11 = (f32[264,512]{1,0:T(8,128)S(1)}, f32[264,512]{1,0:T(8,128)}, u32[]{:S(2)}, u32[]{:S(2)}) collective-permute-start(f32[264,512]{1,0:T(8,128)S(1)} %collective-permute-done.9.refs_3_.refs_11_), channel_id=1, source_target_pairs={{0,8},{1,9},{2,10},{3,11},{4,12},{5,13},{6,14},{7,15},{8,0},{9,1},... | collective-permute-start | bytes 1622024 | tf_op jit(solution)/shard_map/ppermute | solution.py:469
  55.2 36.3 %collective-permute-start.15 = (f32[128,512]{1,0:T(8,128)}, f32[128,512]{1,0:T(8,128)}, u32[]{:S(2)}, u32[]{:S(2)}) collective-permute-start(f32[128,512]{1,0:T(8,128)} %collective-permute-done.13.refs_3_.refs_15_), channel_id=1, source_target_pairs={{0,8},{1,9},{2,10},{3,11},{4,12},{5,13},{6,14},{7,15},{8,0},{9,1},... | collective-permute-start | bytes 786440 | tf_op jit(solution)/shard_map/ppermute | solution.py:478
  57.0 34.5 %collective-permute-start.14 = (f32[136,512]{1,0:T(8,128)S(1)}, f32[136,512]{1,0:T(8,128)}, u32[]{:S(2)}, u32[]{:S(2)}) collective-permute-start(f32[136,512]{1,0:T(8,128)S(1)} %collective-permute-done.12.refs_2_.refs_14_), channel_id=1, source_target_pairs={{0,8},{1,9},{2,10},{3,11},{4,12},{5,13},{6,14},{7,15},{8,0},{9,1},... | collective-permute-start | bytes 835592 | tf_op jit(solution)/shard_map/ppermute | solution.py:476
  61.4 1.6 %copy-start.1 = (f32[2,8,32768]{2,1,0:T(8,128)S(1)}, f32[2,8,32768]{2,1,0:T(8,128)}, u32[]{:S(2)}) copy-start(f32[2,8,32768]{2,1,0:T(8,128)} %param.7) | copy-start | bytes 6291460
  63.0 5.4 %copy-start = (f32[512,512]{1,0:T(8,128)S(1)}, f32[512,512]{1,0:T(8,128)}, u32[]{:S(2)}) copy-start(f32[512,512]{1,0:T(8,128)} %refs_1_.3) | copy-start | bytes 3145732
where the time goes:
time: 135 us; the launch traced here: 137 us
  Pallas kernels  73.5 us (54%)
  waiting for transfers between devices  34.7 us (26%)
  starting transfers between devices  15.4 us (11%)
  local copies, waits for them, and re-layouts  8.42 us (6%)
  other arithmetic  4.44 us (3%)
    pallas_call x1, Pallas kernels, apply(): pl.pallas_call(functools.partial(apply_kernel, nslab, slots, pieces, info...  42.5 us
    ppermute x3, waiting for transfers between devices, gather_pieces(): up = lax.ppermute(up, AXES, onward)  30.2 us
    pallas_call x6, Pallas kernels, project(): pl.pallas_call(functools.partial(project_kernel, local, infos), out_shape...  25.7 us
    pallas_call x1, Pallas kernels, split_bands(): pl.pallas_call(split_bands_kernel, out_shape=jax.ShapeDtypeStruct(shape,...  5.36 us
    ppermute x4, starting transfers between devices, gather_pieces(): lax.ppermute(down, AXES, sibling)  4.89 us
    ppermute x1, waiting for transfers between devices, gather_pieces(): down = lax.ppermute(down[INFO + quarter:], AXES, backward)  4.42 us
    ppermute x3, starting transfers between devices, gather_pieces(): up = lax.ppermute(up, AXES, onward)  4.31 us
    ppermute x3, starting transfers between devices, gather_pieces(): lax.ppermute(up, AXES, sibling)  3.96 us
  transfers between devices with their start and end apart: 16, of which 4 were waited for; matrix products, arithmetic and copies ran while one was open for 5% of the time, Pallas kernels for 21%

commit v1 on v0

--- a/solution.py
+++ b/solution.py
@@ -423,7 +423,7 @@
 Piece = collections.namedtuple("Piece", ["array", "offset", "rows", "info", "index"])
 
 
-def gather_pieces(projectors, described, nband, nslab):
+def gather_and_project(projectors, described, split, extra, nband, nslab):
     slots = projectors.shape[0]
     order, at = cycle_tables(nslab)
     half = slots // 2
@@ -439,46 +439,76 @@
     core = lax.rem(lax.axis_index("band"), 2)
     mine = lax.dynamic_slice_in_dim(projectors, core * half, half, 0)
     mine = jnp.concatenate([described, mine], axis=0)
-    arrays, pieces, calls, infos = [described, projectors], [Piece(1, 0, slots, 0, 0)], [[0]], [(0, 0)]
-    places = [lambda core, slab: (slab, 0)]
-
-    def add(array, distance, start, other, info=None):
+
+    where = [(0, 0, None)]
+    for step in range(1, reach):
+        where += [(1 - step, 0, True), (step - 1, 0, True)] if step > 1 else []
+        where += [(-step, 0, False), (step, 0, False)]
+    where += [(1 - reach, 0, True), (reach - 1, 0, True)]
+    where += [(reach, 0, False), (reach, quarter, False), (reach, 0, True), (reach, quarter, True)]
+    boxes = split.shape[0] // nslab
+
+    def entry(core, slab, distance, start, other):
+        there = order[(at[slab] + distance) % nslab]
+        if other is not None:
+            start += half * ((1 - core) if other else core)
+        return there, start, there * boxes
+
+    table = [[entry(b % 2, s, *w) for w in where] for b in range(nband) for s in range(nslab)]
+    me = lax.axis_index("band") * nslab + lax.axis_index("slab")
+    place = lax.dynamic_index_in_dim(
+        jnp.asarray(np.array(table, np.int32)), me, 0, keepdims=False
+    ).reshape(-1)
+
+    arrays, pieces, infos, projections = [described, projectors], [], [(0, 0)], []
+
+    def add(array, info=None):
         arrays.append(array)
         own = len(arrays) - 1
         offset = INFO if info is None else 0
-        info = own if info is None else info
-        pieces.append(Piece(own, offset, array.shape[0] - offset, info, len(places)))
-        places.append(
-            lambda core, slab: (
-                order[(at[slab] + distance) % nslab],
-                (1 - core if other else core) * half + start,
-            )
+        pieces.append(
+            Piece(own, offset, array.shape[0] - offset, own if info is None else info, len(pieces))
         )
-        return len(pieces) - 1
-
-    waiting = []
-    up = down = mine
-    for step in range(1, reach):
-        up = lax.ppermute(up, AXES, onward)
-        down = lax.ppermute(down, AXES, backward)
-        now = [add(up, -step, 0, False), add(down, step, 0, False)]
-        infos += [(pieces[i].array, pieces[i].index) for i in now]
-        calls.append(now + waiting)
-        waiting = [
-            add(lax.ppermute(up, AXES, sibling), -step, 0, True),
-            add(lax.ppermute(down, AXES, sibling), step, 0, True),
-        ]
-    up = lax.ppermute(up[: INFO + quarter], AXES, onward)
-    down = lax.ppermute(down[INFO + quarter :], AXES, backward)
-    first = add(up, reach, 0, False)
-    infos.append((pieces[first].array, pieces[first].index))
-    calls.append([first, add(down, reach, quarter, False, pieces[first].array)] + waiting)
-    first = add(lax.ppermute(up, AXES, sibling), reach, 0, True)
-    second = add(
-        lax.ppermute(down, AXES, sibling), reach, quarter, True, pieces[first].array
+        return own
+
+    pieces.append(Piece(1, 0, slots, 0, 0))
+    up = lax.ppermute(mine, AXES, onward)
+    down = lax.ppermute(mine, AXES, backward)
+    done = 0
+
+    def project_new():
+        nonlocal done
+        projections.extend(project(arrays, pieces[done:], place, split))
+        done = len(pieces)
+
+    project_new()
+    up, down, projections, place, extra = lax.optimization_barrier(
+        (up, down, projections, place, extra)
     )
-    calls.append([first, second])
-    return arrays, pieces, calls, infos, places
+    projections = list(projections)
+    near = []
+    for step in range(1, reach + 1):
+        last = step == reach
+        for array in near:
+            add(array)
+        for array in (up,) if last else (up, down):
+            infos.append((add(array), len(pieces) - 1))
+        if last:
+            add(down, len(arrays) - 1)
+        near = [lax.ppermute(up, AXES, sibling), lax.ppermute(down, AXES, sibling)]
+        if step + 1 < reach:
+            up = lax.ppermute(up, AXES, onward)
+            down = lax.ppermute(down, AXES, backward)
+        elif not last:
+            up = lax.ppermute(up[: INFO + quarter], AXES, onward)
+            down = lax.ppermute(down[INFO + quarter :], AXES, backward)
+        project_new()
+        up, down, near, projections = lax.optimization_barrier((up, down, near, projections))
+        near, projections = list(near), list(projections)
+    add(near[0])
+    add(near[1], len(arrays) - 1)
+    project_new()
+    return arrays, pieces, infos, projections, place, extra
 
 
 def body(bands, projectors, slot_atom, slot_box, channels, coupling):
@@ -492,15 +522,6 @@
 
     slab = lax.axis_index("slab")
     described = describe(slot_atom, slot_box, slab, nslab, natoms, projectors.shape[1], lanes)
-    arrays, pieces, calls, infos, places = gather_pieces(projectors, described, nband, nslab)
-    table = np.array(
-        [[p(b % 2, s) for p in places] for b in range(nband) for s in range(nslab)], np.int32
-    )
-    boxes = ngrid // BOXPTS // nslab
-    table = np.concatenate([table, table[:, :, :1] * boxes], axis=2)
-    me = lax.axis_index("band") * nslab + slab
-    place = lax.dynamic_index_in_dim(jnp.asarray(table), me, 0, keepdims=False).reshape(-1)
-
     mask = (jnp.arange(channel, dtype=jnp.int32)[:, None] < channels[None, :]).astype(jnp.float32)
     masked = coupling * mask[:, None, :] * mask[None, :, :]
     masked = masked.reshape(channel * channel, nslab, atom_dev).transpose(1, 0, 2)
@@ -512,10 +533,9 @@
     if padded != rows:
         x = jnp.pad(x, ((0, padded - rows), (0, 0)))
     split = split_bands(x)
-    projections = [None] * len(pieces)
-    for call in calls:
-        for i, value in zip(call, project(arrays, [pieces[i] for i in call], place, split)):
-            projections[i] = value
+    arrays, pieces, infos, projections, place, masked = gather_and_project(
+        projectors, described, split, masked, nband, nslab
+    )
     out = apply(arrays, pieces, infos, projections, place, masked, nslab, slots, padded, ngrid)
     return out[:rows].reshape(nblock, band_local, ngrid)
 

time: 135 us -> 107 us (0.79); the launches traced: 137 us -> 106 us
  waiting for transfers between devices: 34.7 us -> 13.1 us
  Pallas kernels: 73.5 us -> 66.1 us
  local copies, waits for them, and re-layouts: 8.42 us -> 3.92 us
  starting transfers between devices: 15.4 us -> 18.8 us
    ppermute x16, waiting for transfers between devices: 34.7 us -> 13.1 us  [the longest x2 8.52 us: gather_and_project(): up = lax.ppermute(up, AXES, onward)]
    pallas_call x6, Pallas kernels: 25.7 us -> 21.5 us  [project(): pl.pallas_call(functools.partial(project_kernel, local, infos), out_shape...]
    ppermute x16, starting transfers between devices: 15.4 us -> 18.8 us  [the longest x8 12.1 us: gather_and_project(): near = [lax.ppermute(up, AXES, sibling), lax.ppermute(down, AXES, sibling)]]
    pallas_call x1, Pallas kernels: 42.5 us -> 39.2 us  [apply(): pl.pallas_call(functools.partial(apply_kernel, nslab, slots, pieces, info...]
    reshape x2, local copies, waits for them, and re-layouts: 2.75 us -> 1.1 us  [body(): masked.reshape(channel * channel, nslab, atom_dev).transpose(1, 0, 2)]
    unnamed x4 -> x8, local copies, waits for them, and re-layouts: 1.59 us -> 0.02 us
    slice x2, local copies, waits for them, and re-layouts: 1.47 us -> 0.04 us  [the longest x1 0.02 us: gather_and_project(): up = lax.ppermute(up[:INFO + quarter], AXES, onward)]
  transfers between devices with their start and end apart: 16 -> 16, of which waited for: 4 -> 6; matrix products, arithmetic and copies ran while one was open for 5% -> 3% of each run, Pallas kernels for 21% -> 23%
where the time goes in v1:
time: 107 us; the launch traced here: 106 us
  Pallas kernels  66.1 us (62%)
  starting transfers between devices  18.8 us (18%)
  waiting for transfers between devices  13.1 us (12%)
  local copies, waits for them, and re-layouts  3.92 us (4%)
  other arithmetic  3.65 us (3%)
    pallas_call x1, Pallas kernels, apply(): pl.pallas_call(functools.partial(apply_kernel, nslab, slots, pieces, info...  39.2 us
    pallas_call x6, Pallas kernels, project(): pl.pallas_call(functools.partial(project_kernel, local, infos), out_shape...  21.5 us
    ppermute x8, starting transfers between devices, gather_and_project(): near = [lax.ppermute(up, AXES, sibling), lax.ppermute(down, AXES, sibling)]  12.1 us
    ppermute x2, waiting for transfers between devices, gather_and_project(): up = lax.ppermute(up, AXES, onward)  8.52 us
    pallas_call x1, Pallas kernels, split_bands(): pl.pallas_call(split_bands_kernel, out_shape=jax.ShapeDtypeStruct(shape,...  5.36 us
    ppermute x2, starting transfers between devices, gather_and_project(): up = lax.ppermute(up, AXES, onward)  2.59 us
  transfers between devices with their start and end apart: 16, of which 6 were waited for; matrix products, arithmetic and copies ran while one was open for 3% of the time, Pallas kernels for 23%

profile of v1, /device:TPU:1, one launch (start us, length us, event | category | flops | bytes accessed | tf_op | source)
XLA Modules:
  0.0 105.7 jit_solution(2670222215039259042)
XLA Ops:
  0.0 1.4 %convert_reduce_fusion = (s32[]{:T(128)}, s32[512]{0:T(512)S(1)}) fusion(s32[512]{0:T(512)} %param.9, s32[]{:T(128)S(6)} %mul.25), kind=kLoop, calls=%fused_computation.10 | loop fusion | flops 7167 | bytes 4104 | tf_op jit(solution)/shard_map/reduce_sum | solution.py:99
  2.1 1.2 %constant_dynamic-slice_fusion.1 = f32[256,512]{1,0:T(8,128)S(1)} fusion(f32[512,512]{1,0:T(8,128)} %refs_1_.3, s32[]{:T(128)S(6)} %select_n.32), kind=kLoop, calls=%fused_computation.13 | loop fusion | bytes 1048580 | tf_op jit(solution)/shard_map/dynamic_slice | solution.py:440
  4.9 2.1 %collective-permute-start = (f32[264,512]{1,0:T(8,128)}, f32[264,512]{1,0:T(8,128)S(1)}, u32[]{:S(2)}, u32[]{:S(2)}) collective-permute-start(f32[264,512]{1,0:T(8,128)} %pad_maximum_fusion), channel_id=1, source_target_pairs={{0,2},{2,4},{4,6},{6,7},{7,5},{5,3},{3,1},{1,0},{8,10},{10,12},{12... | collective-permute-start | bytes 1622024 | tf_op jit(solution)/shard_map/ppermute | solution.py:475
  8.6 1.1 reshape.53
  9.7 5.4 %split_bands.1.x_ref = bf16[512,16,256]{2,1,0:T(8,128)(2,1)S(1)} custom-call(f32[16,32768]{1,0:T(8,128)S(1)} %bitcast.8), custom_call_target="tpu_custom_call" | custom-call | flops 4194304 | bytes 6291456 | tf_op jit(solution)/shard_map/split_bands/pallas_call | solution.py:63
  15.1 4.4 %project.6.refs_18_ = f32[32,16,128]{2,1,0:T(8,128)S(1)} custom-call(s32[51]{0:T(128)S(1)} %reshape.51.place_ref, bf16[512,16,256]{2,1,0:T(8,128)(2,1)S(1)} %split_bands.1.x_ref, f32[8,512]{1,0:T(8,128)S(1)} %pad.8.refs_0_, f32[512,512]{1,0:T(8,128)S(1)} %copy-done), custom_call_target="tpu_custom_call" | custom-call | flops 134217728 | bytes 5242880 | tf_op jit(solution)/shard_map/project/pallas_call | solution.py:165
  20.1 1.3 %collective-permute-start.2 = (f32[264,512]{1,0:T(8,128)S(1)}, f32[264,512]{1,0:T(8,128)S(1)}, u32[]{:S(2)}, u32[]{:S(2)}) collective-permute-start(f32[264,512]{1,0:T(8,128)S(1)} %collective-permute-done.refs_0_.refs_2_), channel_id=1, source_target_pairs={{0,2},{2,4},{4,6},{6,7},{7,5},{5,3},{3,1},{1,0},{8,10},{10,12},{12... | collective-permute-start | bytes 1622024 | tf_op jit(solution)/shard_map/ppermute | solution.py:500
  21.5 2.4 %collective-permute-start.4 = (f32[264,512]{1,0:T(8,128)S(1)}, f32[264,512]{1,0:T(8,128)S(1)}, u32[]{:S(2)}, u32[]{:S(2)}) collective-permute-start(f32[264,512]{1,0:T(8,128)S(1)} %collective-permute-done.refs_0_.refs_2_), channel_id=1, source_target_pairs={{0,8},{1,9},{2,10},{3,11},{4,12},{5,13},{6,14},{7,15},{8,0},{9,1},... | collective-permute-start | bytes 1622024 | tf_op jit(solution)/shard_map/ppermute | solution.py:498
  24.0 1.7 %project.7 = (f32[16,16,128]{2,1,0:T(8,128)S(1)}, f32[16,16,128]{2,1,0:T(8,128)S(1)}) custom-call(s32[51]{0:T(128)S(1)} %reshape.51.place_ref, bf16[512,16,256]{2,1,0:T(8,128)(2,1)S(1)} %split_bands.1.x_ref, f32[264,512]{1,0:T(8,128)S(1)} %collective-permute-done.refs_0_.refs_2_, f32[264,512]{1,0:T(8,128)S(1)} %collective-permute-done.1.refs_1_.refs_3_), custom_call_target="tpu_custom_call" | custom-call | flops 134217728 | bytes 5242880 | tf_op jit(solution)/shard_map/project/pallas_call | solution.py:165
  25.7 6.3 %collective-permute-done.2.refs_2_.refs_6_ = f32[264,512]{1,0:T(8,128)S(1)} collective-permute-done((f32[264,512]{1,0:T(8,128)S(1)}, f32[264,512]{1,0:T(8,128)S(1)}, u32[]{:S(2)}, u32[]{:S(2)}) %collective-permute-start.2) | collective-permute-done | bytes 540704 | tf_op jit(solution)/shard_map/ppermute | solution.py:500
  32.0 1.0 collective-permute-done.3.refs_3_.refs_7_
  33.0 1.3 %collective-permute-start.6 = (f32[264,512]{1,0:T(8,128)S(1)}, f32[264,512]{1,0:T(8,128)S(1)}, u32[]{:S(2)}, u32[]{:S(2)}) collective-permute-start(f32[264,512]{1,0:T(8,128)S(1)} %collective-permute-done.2.refs_2_.refs_6_), channel_id=1, source_target_pairs={{0,2},{2,4},{4,6},{6,7},{7,5},{5,3},{3,1},{1,0},{8,10},{10,12},{12... | collective-permute-start | bytes 1622024 | tf_op jit(solution)/shard_map/ppermute | solution.py:500
  34.5 3.6 %collective-permute-start.8 = (f32[264,512]{1,0:T(8,128)S(1)}, f32[264,512]{1,0:T(8,128)S(1)}, u32[]{:S(2)}, u32[]{:S(2)}) collective-permute-start(f32[264,512]{1,0:T(8,128)S(1)} %collective-permute-done.2.refs_2_.refs_6_), channel_id=1, source_target_pairs={{0,8},{1,9},{2,10},{3,11},{4,12},{5,13},{6,14},{7,15},{8,0},{9,1},... | collective-permute-start | bytes 1622024 | tf_op jit(solution)/shard_map/ppermute | solution.py:498
  38.1 3.4 %project.8 = (f32[16,16,128]{2,1,0:T(8,128)S(1)}, f32[16,16,128]{2,1,0:T(8,128)S(1)}, f32[16,16,128]{2,1,0:T(8,128)S(1)}, f32[16,16,128]{2,1,0:T(8,128)S(1)}) custom-call(s32[51]{0:T(128)S(1)} %reshape.51.place_ref, bf16[512,16,256]{2,1,0:T(8,128)(2,1)S(1)} %split_bands.1.x_ref, f32[264,512]{1,0:T(8,128)S(1)} %collective-permute-done.4.refs_0_.refs_4_, ...), custom_call_target="tpu_custom_call" | custom-call | flops 268435456 | bytes 6291456 | tf_op jit(solution)/shard_map/project/pallas_call | solution.py:165
  41.5 2.2 %collective-permute-done.6.refs_2_.refs_10_ = f32[264,512]{1,0:T(8,128)S(1)} collective-permute-done((f32[264,512]{1,0:T(8,128)S(1)}, f32[264,512]{1,0:T(8,128)S(1)}, u32[]{:S(2)}, u32[]{:S(2)}) %collective-permute-start.6) | collective-permute-done | bytes 540704 | tf_op jit(solution)/shard_map/ppermute | solution.py:500
  43.7 1.0 collective-permute-done.7.refs_3_.refs_11_
  44.7 4.3 %collective-permute-start.12 = (f32[264,512]{1,0:T(8,128)S(1)}, f32[264,512]{1,0:T(8,128)S(1)}, u32[]{:S(2)}, u32[]{:S(2)}) collective-permute-start(f32[264,512]{1,0:T(8,128)S(1)} %collective-permute-done.6.refs_2_.refs_10_), channel_id=1, source_target_pairs={{0,8},{1,9},{2,10},{3,11},{4,12},{5,13},{6,14},{7,15},{8,0},{9,1},... | collective-permute-start | bytes 1622024 | tf_op jit(solution)/shard_map/ppermute | solution.py:498
  49.1 1.3 %collective-permute-start.10 = (f32[136,512]{1,0:T(8,128)S(1)}, f32[136,512]{1,0:T(8,128)S(1)}, u32[]{:S(2)}, u32[]{:S(2)}) collective-permute-start(f32[136,512]{1,0:T(8,128)S(1)} %slice.6), channel_id=1, source_target_pairs={{0,2},{2,4},{4,6},{6,7},{7,5},{5,3},{3,1},{1,0},{8,10},{10,12},{12... | collective-permute-start | bytes 835592 | tf_op jit(solution)/shard_map/ppermute | solution.py:503
  50.7 4.9 %project.9 = (f32[16,16,128]{2,1,0:T(8,128)S(1)}, f32[16,16,128]{2,1,0:T(8,128)S(1)}, f32[16,16,128]{2,1,0:T(8,128)S(1)}, f32[16,16,128]{2,1,0:T(8,128)S(1)}) custom-call(s32[51]{0:T(128)S(1)} %reshape.51.place_ref, bf16[512,16,256]{2,1,0:T(8,128)(2,1)S(1)} %split_bands.1.x_ref, f32[264,512]{1,0:T(8,128)S(1)} %collective-permute-done.8.refs_0_.refs_8_, ...), custom_call_target="tpu_custom_call" | custom-call | flops 268435456 | bytes 6291456 | tf_op jit(solution)/shard_map/project/pallas_call | solution.py:165
  55.6 1.9 %collective-permute-done.11.refs_3_.refs_15_ = f32[128,512]{1,0:T(8,128)S(1)} collective-permute-done((f32[128,512]{1,0:T(8,128)S(1)}, f32[128,512]{1,0:T(8,128)S(1)}, u32[]{:S(2)}, u32[]{:S(2)}) %collective-permute-start.11) | collective-permute-done | bytes 262176 | tf_op jit(solution)/shard_map/ppermute | solution.py:504
  57.6 1.7 %collective-permute-start.14 = (f32[136,512]{1,0:T(8,128)S(1)}, f32[136,512]{1,0:T(8,128)S(1)}, u32[]{:S(2)}, u32[]{:S(2)}) collective-permute-start(f32[136,512]{1,0:T(8,128)S(1)} %collective-permute-done.10.refs_2_.refs_14_), channel_id=1, source_target_pairs={{0,8},{1,9},{2,10},{3,11},{4,12},{5,13},{6,14},{7,15},{8,0},{9,1},... | collective-permute-start | bytes 835592 | tf_op jit(solution)/shard_map/ppermute | solution.py:498
  59.3 5.0 %project.10 = (f32[16,16,128]{2,1,0:T(8,128)S(1)}, f32[16,16,128]{2,1,0:T(8,128)S(1)}, f32[8,16,128]{2,1,0:T(8,128)S(1)}, f32[8,16,128]{2,1,0:T(8,128)S(1)}) custom-call(s32[51]{0:T(128)S(1)} %reshape.51.place_ref, bf16[512,16,256]{2,1,0:T(8,128)(2,1)S(1)} %split_bands.1.x_ref, f32[264,512]{1,0:T(8,128)S(1)} %collective-permute-done.12.refs_0_.refs_12_, ...), custom_call_target="tpu_custom_call" | custom-call | flops 201326592 | bytes 5767168 | tf_op jit(solution)/shard_map/project/pallas_call | solution.py:165
  64.3 2.1 %project.11 = (f32[8,16,128]{2,1,0:T(8,128)S(1)}, f32[8,16,128]{2,1,0:T(8,128)S(1)}) custom-call(s32[51]{0:T(128)S(1)} %reshape.51.place_ref, bf16[512,16,256]{2,1,0:T(8,128)(2,1)S(1)} %split_bands.1.x_ref, f32[136,512]{1,0:T(8,128)S(1)} %collective-permute-done.14.refs_0_.refs_16_, f32[128,512]{1,0:T(8,128)S(1)} %collective-permute-done.15.refs_1_.refs_17_), custom_call_target="tpu_custom_call" | custom-call | flops 67108864 | bytes 4718592 | tf_op jit(solution)/shard_map/project/pallas_call | solution.py:165
  66.5 39.2 %apply.1 = f32[16,32768]{1,0:T(8,128)} custom-call(s32[51]{0:T(128)S(1)} %reshape.51.place_ref, f32[8,64,128]{2,1,0:T(8,128)S(1)} %pad.9.coupling_ref, f32[8,512]{1,0:T(8,128)S(1)} %pad.8.refs_0_, f32[512,512]{1,0:T(8,128)S(1)} %copy-done, f32[264,512]{1,0:T(8,128)S(1)} %collective-permute-done.refs_0_.refs_2_, ...), custom_call_target="tpu_custom_call" | custom-call | tf_op jit(solution)/shard_map/apply/pallas_call | solution.py:412
  (39 shorter events, 5.3 us)
Async XLA Ops:
  0.0 7.8 %copy-start.3 = (s32[768]{0:T(1024)S(1)}, s32[768]{0:T(1024)}, u32[]{:S(2)}) copy-start(s32[768]{0:T(1024)} %param.11) | copy-start | bytes 9220
  0.0 7.9 %copy-start.2 = (f32[8,8,768]{2,1,0:T(8,128)S(1)}, f32[8,8,768]{2,1,0:T(8,128)}, u32[]{:S(2)}) copy-start(f32[8,8,768]{2,1,0:T(8,128)} %param.12) | copy-start | bytes 589828
  2.1 7.6 %copy-start.1 = (f32[2,8,32768]{2,1,0:T(8,128)S(1)}, f32[2,8,32768]{2,1,0:T(8,128)}, u32[]{:S(2)}) copy-start(f32[2,8,32768]{2,1,0:T(8,128)} %param.7) | copy-start | bytes 6291460
  4.9 14.6 %collective-permute-start = (f32[264,512]{1,0:T(8,128)}, f32[264,512]{1,0:T(8,128)S(1)}, u32[]{:S(2)}, u32[]{:S(2)}) collective-permute-start(f32[264,512]{1,0:T(8,128)} %pad_maximum_fusion), channel_id=1, source_target_pairs={{0,2},{2,4},{4,6},{6,7},{7,5},{5,3},{3,1},{1,0},{8,10},{10,12},{12... | collective-permute-start | bytes 1622024 | tf_op jit(solution)/shard_map/ppermute | solution.py:475
  7.0 13.0 %collective-permute-start.1 = (f32[264,512]{1,0:T(8,128)}, f32[264,512]{1,0:T(8,128)S(1)}, u32[]{:S(2)}, u32[]{:S(2)}) collective-permute-start(f32[264,512]{1,0:T(8,128)} %pad_maximum_fusion), channel_id=1, source_target_pairs={{2,0},{4,2},{6,4},{7,6},{5,7},{3,5},{1,3},{0,1},{10,8},{12,10},{14... | collective-permute-start | bytes 1622024 | tf_op jit(solution)/shard_map/ppermute | solution.py:476
  9.7 5.4 %copy-start = (f32[512,512]{1,0:T(8,128)S(1)}, f32[512,512]{1,0:T(8,128)}, u32[]{:S(2)}) copy-start(f32[512,512]{1,0:T(8,128)} %refs_1_.3) | copy-start | bytes 3145732
  20.1 11.9 %collective-permute-start.2 = (f32[264,512]{1,0:T(8,128)S(1)}, f32[264,512]{1,0:T(8,128)S(1)}, u32[]{:S(2)}, u32[]{:S(2)}) collective-permute-start(f32[264,512]{1,0:T(8,128)S(1)} %collective-permute-done.refs_0_.refs_2_), channel_id=1, source_target_pairs={{0,2},{2,4},{4,6},{6,7},{7,5},{5,3},{3,1},{1,0},{8,10},{10,12},{12... | collective-permute-start | bytes 1622024 | tf_op jit(solution)/shard_map/ppermute | solution.py:500
  21.4 11.6 %collective-permute-start.3 = (f32[264,512]{1,0:T(8,128)S(1)}, f32[264,512]{1,0:T(8,128)S(1)}, u32[]{:S(2)}, u32[]{:S(2)}) collective-permute-start(f32[264,512]{1,0:T(8,128)S(1)} %collective-permute-done.1.refs_1_.refs_3_), channel_id=1, source_target_pairs={{2,0},{4,2},{6,4},{7,6},{5,7},{3,5},{1,3},{0,1},{10,8},{12,10},{14... | collective-permute-start | bytes 1622024 | tf_op jit(solution)/shard_map/ppermute | solution.py:501
  21.5 11.5 %collective-permute-start.4 = (f32[264,512]{1,0:T(8,128)S(1)}, f32[264,512]{1,0:T(8,128)S(1)}, u32[]{:S(2)}, u32[]{:S(2)}) collective-permute-start(f32[264,512]{1,0:T(8,128)S(1)} %collective-permute-done.refs_0_.refs_2_), channel_id=1, source_target_pairs={{0,8},{1,9},{2,10},{3,11},{4,12},{5,13},{6,14},{7,15},{8,0},{9,1},... | collective-permute-start | bytes 1622024 | tf_op jit(solution)/shard_map/ppermute | solution.py:498
  24.0 9.0 %collective-permute-start.5 = (f32[264,512]{1,0:T(8,128)S(1)}, f32[264,512]{1,0:T(8,128)S(1)}, u32[]{:S(2)}, u32[]{:S(2)}) collective-permute-start(f32[264,512]{1,0:T(8,128)S(1)} %collective-permute-done.1.refs_1_.refs_3_), channel_id=1, source_target_pairs={{0,8},{1,9},{2,10},{3,11},{4,12},{5,13},{6,14},{7,15},{8,0},{9,1},... | collective-permute-start | bytes 1622024 | tf_op jit(solution)/shard_map/ppermute | solution.py:498
  33.0 10.7 %collective-permute-start.6 = (f32[264,512]{1,0:T(8,128)S(1)}, f32[264,512]{1,0:T(8,128)S(1)}, u32[]{:S(2)}, u32[]{:S(2)}) collective-permute-start(f32[264,512]{1,0:T(8,128)S(1)} %collective-permute-done.2.refs_2_.refs_6_), channel_id=1, source_target_pairs={{0,2},{2,4},{4,6},{6,7},{7,5},{5,3},{3,1},{1,0},{8,10},{10,12},{12... | collective-permute-start | bytes 1622024 | tf_op jit(solution)/shard_map/ppermute | solution.py:500
  34.3 10.4 %collective-permute-start.7 = (f32[264,512]{1,0:T(8,128)S(1)}, f32[264,512]{1,0:T(8,128)S(1)}, u32[]{:S(2)}, u32[]{:S(2)}) collective-permute-start(f32[264,512]{1,0:T(8,128)S(1)} %collective-permute-done.3.refs_3_.refs_7_), channel_id=1, source_target_pairs={{2,0},{4,2},{6,4},{7,6},{5,7},{3,5},{1,3},{0,1},{10,8},{12,10},{14... | collective-permute-start | bytes 1622024 | tf_op jit(solution)/shard_map/ppermute | solution.py:501
  34.5 10.3 %collective-permute-start.8 = (f32[264,512]{1,0:T(8,128)S(1)}, f32[264,512]{1,0:T(8,128)S(1)}, u32[]{:S(2)}, u32[]{:S(2)}) collective-permute-start(f32[264,512]{1,0:T(8,128)S(1)} %collective-permute-done.2.refs_2_.refs_6_), channel_id=1, source_target_pairs={{0,8},{1,9},{2,10},{3,11},{4,12},{5,13},{6,14},{7,15},{8,0},{9,1},... | collective-permute-start | bytes 1622024 | tf_op jit(solution)/shard_map/ppermute | solution.py:498
  38.1 6.6 %collective-permute-start.9 = (f32[264,512]{1,0:T(8,128)S(1)}, f32[264,512]{1,0:T(8,128)S(1)}, u32[]{:S(2)}, u32[]{:S(2)}) collective-permute-start(f32[264,512]{1,0:T(8,128)S(1)} %collective-permute-done.3.refs_3_.refs_7_), channel_id=1, source_target_pairs={{0,8},{1,9},{2,10},{3,11},{4,12},{5,13},{6,14},{7,15},{8,0},{9,1},... | collective-permute-start | bytes 1622024 | tf_op jit(solution)/shard_map/ppermute | solution.py:498
  44.7 12.8 %collective-permute-start.12 = (f32[264,512]{1,0:T(8,128)S(1)}, f32[264,512]{1,0:T(8,128)S(1)}, u32[]{:S(2)}, u32[]{:S(2)}) collective-permute-start(f32[264,512]{1,0:T(8,128)S(1)} %collective-permute-done.6.refs_2_.refs_10_), channel_id=1, source_target_pairs={{0,8},{1,9},{2,10},{3,11},{4,12},{5,13},{6,14},{7,15},{8,0},{9,1},... | collective-permute-start | bytes 1622024 | tf_op jit(solution)/shard_map/ppermute | solution.py:498
  49.0 8.6 %collective-permute-start.13 = (f32[264,512]{1,0:T(8,128)S(1)}, f32[264,512]{1,0:T(8,128)S(1)}, u32[]{:S(2)}, u32[]{:S(2)}) collective-permute-start(f32[264,512]{1,0:T(8,128)S(1)} %collective-permute-done.7.refs_3_.refs_11_), channel_id=1, source_target_pairs={{0,8},{1,9},{2,10},{3,11},{4,12},{5,13},{6,14},{7,15},{8,0},{9,1},... | collective-permute-start | bytes 1622024 | tf_op jit(solution)/shard_map/ppermute | solution.py:498
  49.1 8.5 %collective-permute-start.10 = (f32[136,512]{1,0:T(8,128)S(1)}, f32[136,512]{1,0:T(8,128)S(1)}, u32[]{:S(2)}, u32[]{:S(2)}) collective-permute-start(f32[136,512]{1,0:T(8,128)S(1)} %slice.6), channel_id=1, source_target_pairs={{0,2},{2,4},{4,6},{6,7},{7,5},{5,3},{3,1},{1,0},{8,10},{10,12},{12... | collective-permute-start | bytes 835592 | tf_op jit(solution)/shard_map/ppermute | solution.py:503
  50.4 7.2 %collective-permute-start.11 = (f32[128,512]{1,0:T(8,128)S(1)}, f32[128,512]{1,0:T(8,128)S(1)}, u32[]{:S(2)}, u32[]{:S(2)}) collective-permute-start(f32[128,512]{1,0:T(8,128)S(1)} %slice.7), channel_id=1, source_target_pairs={{2,0},{4,2},{6,4},{7,6},{5,7},{3,5},{1,3},{0,1},{10,8},{12,10},{14... | collective-permute-start | bytes 786440 | tf_op jit(solution)/shard_map/ppermute | solution.py:504
  57.6 6.8 %collective-permute-start.14 = (f32[136,512]{1,0:T(8,128)S(1)}, f32[136,512]{1,0:T(8,128)S(1)}, u32[]{:S(2)}, u32[]{:S(2)}) collective-permute-start(f32[136,512]{1,0:T(8,128)S(1)} %collective-permute-done.10.refs_2_.refs_14_), channel_id=1, source_target_pairs={{0,8},{1,9},{2,10},{3,11},{4,12},{5,13},{6,14},{7,15},{8,0},{9,1},... | collective-permute-start | bytes 835592 | tf_op jit(solution)/shard_map/ppermute | solution.py:498
  59.2 5.1 %collective-permute-start.15 = (f32[128,512]{1,0:T(8,128)S(1)}, f32[128,512]{1,0:T(8,128)S(1)}, u32[]{:S(2)}, u32[]{:S(2)}) collective-permute-start(f32[128,512]{1,0:T(8,128)S(1)} %collective-permute-done.11.refs_3_.refs_15_), channel_id=1, source_target_pairs={{0,8},{1,9},{2,10},{3,11},{4,12},{5,13},{6,14},{7,15},{8,0},{9,1},... | collective-permute-start | bytes 786440 | tf_op jit(solution)/shard_map/ppermute | solution.py:498

commit v2 on v1

--- a/solution.py
+++ b/solution.py
@@ -91,31 +91,65 @@
     return lax.div(jnp.clip(live - start, 0, length) + (GROUP - 1), GROUP)
 
 
-def describe(slot_atom, slot_box, slab, nslab, natoms, width, lanes):
+def begin_kernel(natoms, lanes, atom_ref, box_ref, projector_ref, info_ref, mine_ref, info_sem, half_sem):
+    nslab = lax.axis_size("slab")
+    half = mine_ref.shape[0] - INFO
+    core = lax.rem(lax.axis_index("band"), 2)
+    copy = pltpu.make_async_copy(
+        projector_ref.at[pl.ds(pl.multiple_of(core * half, GROUP), half), :],
+        mine_ref.at[pl.ds(INFO, half), :],
+        half_sem,
+    )
+    copy.start()
     atom_dev = natoms // nslab
-    relative = (slot_atom - (slab + nslab - 1) % nslab * atom_dev) % natoms
+    below = lax.rem(lax.axis_index("slab") + nslab - 1, nslab) * atom_dev
+    atom = atom_ref[...]
+    slots = atom.shape[1]
+    relative = atom - below
+    relative = jnp.where(relative < 0, relative + natoms, relative)
     column = jnp.where(relative < atom_dev, relative, relative + (lanes - atom_dev))
-    column = jnp.where(slot_atom >= 0, column, -1)
-    live = jnp.broadcast_to(jnp.sum((slot_atom >= 0).astype(jnp.int32)), slot_atom.shape)
-    rows = jnp.stack([slot_box, live, column]).astype(jnp.float32)
-    return jnp.pad(rows, ((0, INFO - rows.shape[0]), (0, width - rows.shape[1])))
+    live = jnp.sum(jnp.where(atom >= 0, 1.0, 0.0), axis=1, keepdims=True)
+    info_ref[...] = jnp.zeros(info_ref.shape, jnp.float32)
+    info_ref[0:1, 0:slots] = box_ref[...].astype(jnp.float32)
+    info_ref[1:2, 0:slots] = jnp.broadcast_to(live, (1, slots))
+    info_ref[2:3, 0:slots] = jnp.where(atom >= 0, column, -1).astype(jnp.float32)
+    head = pltpu.make_async_copy(info_ref, mine_ref.at[pl.ds(0, INFO), :], info_sem)
+    head.start()
+    head.wait()
+    copy.wait()
+
+
+def begin(slot_atom, slot_box, projectors, natoms, lanes):
+    slots, depth = projectors.shape
+    return pl.pallas_call(
+        functools.partial(begin_kernel, natoms, lanes),
+        out_shape=[
+            jax.ShapeDtypeStruct((INFO, depth), jnp.float32),
+            jax.ShapeDtypeStruct((INFO + slots // 2, depth), jnp.float32),
+        ],
+        in_specs=[VMEM, VMEM, ANY],
+        out_specs=[VMEM, ANY],
+        scratch_shapes=[pltpu.SemaphoreType.DMA(()), pltpu.SemaphoreType.DMA(())],
+        compiler_params=params(8 * MIB),
+        name="begin",
+    )(slot_atom.reshape(1, slots), slot_box.reshape(1, slots), projectors)
 
 
 def project_kernel(pieces, infos, place_ref, x_ref, *refs):
-    arrays = refs[: -len(pieces) - 3]
-    outs = refs[-len(pieces) - 3 : -3]
-    whole, table, sem = refs[-3:]
+    arrays = refs[: -len(pieces) - 4]
+    outs = refs[-len(pieces) - 4 : -4]
+    whole, proj, table, sem = refs[-4:]
     copies = []
     for k, index in enumerate(infos):
         whole[k] = arrays[index][0:INFO, :].astype(jnp.int32)
         copies.append(pltpu.make_async_copy(whole.at[k], table.at[k], sem.at[k]))
         copies[-1].start()
     rows = x_ref.shape[1]
-    width = outs[0].shape[2]
+    width = proj.shape[2]
+    chunk = width // GROUP
+    lane_block = lax.broadcasted_iota(jnp.int32, (rows, width), 1) // GROUP
     low_half = lax.broadcasted_iota(jnp.int32, (GROUP, 128), 1) < BOXPTS
     lane_slot = lax.broadcasted_iota(jnp.int32, (rows, width), 1) % GROUP
-    for out in outs:
-        out[...] = jnp.zeros(out.shape, jnp.float32)
     for c in copies:
         c.wait()
     for p, out in zip(pieces, outs):
@@ -143,13 +177,42 @@
                     total = jnp.where(lane_slot == s, product[s * rows : (s + 1) * rows], total)
                 totals.append(total)
             for g, total in zip(groups, totals):
-                out[g] = total
+                proj[g] = total
             return carry
 
+        proj[...] = jnp.zeros(proj.shape, jnp.float32)
         lax.fori_loop(0, lax.div(count + (UNROLL - 1), UNROLL), step, 0)
 
-
-def project(arrays, pieces, place, x):
+        @pl.when(count == 0)
+        def _():
+            out[...] = jnp.zeros(out.shape, jnp.float32)
+
+        @pl.when(count > 0)
+        def _():
+            columns = arrays[p.info][2:3, :]
+            columns = pltpu.roll(columns, lax.rem(columns.shape[1] - start, columns.shape[1]), 1)
+            nchunk = (p.rows // GROUP + chunk - 1) // chunk
+            value = jnp.concatenate(
+                [
+                    jnp.concatenate(
+                        swap_blocks([proj[k * chunk + i] for i in range(chunk)], lane_block, width),
+                        axis=0,
+                    )
+                    for k in range(nchunk)
+                ],
+                axis=1,
+            )
+            both = lax.dot_general(
+                stacked_split(value),
+                selector(columns[:, : nchunk * width], out.shape[1]),
+                (((1,), (1,)), ((), ())),
+                preferred_element_type=jnp.float32,
+            )
+            half = both.shape[0] // 2
+            out[...] = both[:half] + both[half:]
+
+
+def project(arrays, pieces, place, x, lanes):
     channel = arrays[0].shape[1] // BOXPTS
     used = sorted({p.array for p in pieces} | {p.info for p in pieces})
     local = [
@@ -157,11 +220,11 @@
     ]
     infos = sorted({p.info for p in local})
     shapes = [
-        jax.ShapeDtypeStruct((p.rows // GROUP, x.shape[1], channel * GROUP), jnp.float32)
-        for p in pieces
+        jax.ShapeDtypeStruct((channel * x.shape[1], 2 * lanes), jnp.float32) for p in pieces
     ]
     size = sum(p.rows for p in pieces) * arrays[0].shape[1]
     table = (len(infos), INFO, arrays[0].shape[1])
+    groups = round_up(max(p.rows for p in pieces), channel * GROUP) // GROUP
     return pl.pallas_call(
         functools.partial(project_kernel, local, infos),
         out_shape=shapes,
@@ -169,6 +232,7 @@
         out_specs=[VMEM] * len(pieces),
         scratch_shapes=[
             pltpu.VMEM(table, jnp.int32),
+            pltpu.VMEM((groups, x.shape[1], channel * GROUP), jnp.float32),
             pltpu.SMEM(table, jnp.int32),
             pltpu.SemaphoreType.DMA((len(infos),)),
         ],
@@ -194,6 +258,12 @@
     return tiles
 
 
+def selector(columns, count):
+    shape = (count, columns.shape[1])
+    row = lax.broadcasted_iota(jnp.int32, shape, 0).astype(jnp.float32)
+    return jnp.where(jnp.broadcast_to(columns, shape) == row, 1.0, 0.0).astype(jnp.bfloat16)
+
+
 def stacked_split(value):
     high = value.astype(jnp.bfloat16)
     low = (value - high.astype(jnp.float32)).astype(jnp.bfloat16)
@@ -202,11 +272,11 @@
 
 def apply_kernel(nslab, slots, pieces, infos, place_ref, coupling_ref, *refs):
     npiece = len(pieces)
-    proj, parts, beta, sums, done, masks, info, whole, table = refs[-13:-4]
+    proj, loaded, parts, beta, sums, done, masks, info, whole, table = refs[-14:-4]
     beta_sem, proj_sem, info_sem, out_sem = refs[-4:]
-    out_ref = refs[-14]
-    projections = refs[-14 - npiece : -14]
-    arrays = refs[: -14 - npiece]
+    out_ref = refs[-15]
+    projections = refs[-15 - npiece : -15]
+    arrays = refs[: -15 - npiece]
     groups = slots // GROUP
     rows, width = proj.shape[1], proj.shape[2]
     channel = width // GROUP
@@ -221,11 +291,9 @@
         )
     for i, p in enumerate(pieces):
         slab, start = place_ref[3 * p.index], place_ref[3 * p.index + 1]
-        first = slab * groups + lax.div(start, GROUP)
+        j = i % loaded.shape[0]
         copies.append(
-            pltpu.make_async_copy(
-                projections[i], proj.at[pl.ds(first, p.rows // GROUP)], proj_sem.at[i]
-            )
+            pltpu.make_async_copy(projections[i], loaded.at[j], proj_sem.at[i])
         )
         first = pl.multiple_of(slab * slots + start, GROUP)
         beta_copies.append(
@@ -235,54 +303,31 @@
                 beta_sem.at[i],
             )
         )
-    for c in info_copies + copies + beta_copies:
+    for c in info_copies + copies[: loaded.shape[0]] + beta_copies:
         c.start()
     lane_slot = lax.broadcasted_iota(jnp.int32, (rows, width), 1) % GROUP
     for s in range(GROUP):
         masks[s] = jnp.where(lane_slot == s, 1.0, 0.0).astype(jnp.bfloat16)
+    for j in range(sums.shape[0]):
+        sums[j] = jnp.zeros(sums.shape[1:], jnp.float32)
+    parts[...] = jnp.zeros(parts.shape, jnp.float32)
     for c in info_copies:
         c.wait()
     whole[...] = info[...].astype(jnp.int32)
     to_scalars = pltpu.make_async_copy(whole, table, info_sem.at[0])
     to_scalars.start()
-    for j in range(sums.shape[0]):
-        sums[j] = jnp.zeros(sums.shape[1:], jnp.float32)
-    parts[...] = jnp.zeros(parts.shape, jnp.float32)
-    to_scalars.wait()
-    for c in copies:
-        c.wait()
+    for first in range(0, npiece, loaded.shape[0]):
+        wave = range(first, min(first + loaded.shape[0], npiece))
+        for i in wave:
+            if first > 0:
+                copies[i].start()
+        for i in wave:
+            copies[i].wait()
+        for i in wave:
+            slab = place_ref[3 * pieces[i].index]
+            parts[slab] = parts[slab] + loaded[i % loaded.shape[0]]
 
     lane_block = lax.broadcasted_iota(jnp.int32, (rows, width), 1) // GROUP
-    atom_row = lax.broadcasted_iota(jnp.int32, (2 * lanes, width), 0).astype(jnp.float32)
-
-    def selector(slab, k):
-        first = pl.multiple_of(k * width, 128)
-        column = jnp.broadcast_to(info[slab, 2:3, pl.ds(first, width)], (2 * lanes, width))
-        return jnp.where(column == atom_row, 1.0, 0.0).astype(jnp.bfloat16)
-
-    def chunks(slab):
-        return lax.div(table[slab, 1, 0] + (width - 1), width)
-
-    def sum_by_atom(slab, carry):
-        def step(k, inner):
-            first = slab * groups + k * chunk
-            tiles = [proj[first + i] for i in range(chunk)]
-            value = jnp.concatenate(swap_blocks(tiles, lane_block, width), axis=0)
-            both = lax.dot_general(
-                stacked_split(value),
-                selector(slab, k),
-                (((1,), (1,)), ((), ())),
-                preferred_element_type=jnp.float32,
-            )
-            half = both.shape[0] // 2
-            parts[slab] = parts[slab] + (both[:half] + both[half:])
-            return inner
-
-        lax.fori_loop(0, chunks(slab), step, 0)
-        return carry
-
-    lax.fori_loop(0, nslab, sum_by_atom, 0)
-
     def couple(slab, carry):
         following = lax.rem(slab + 1, nslab)
         total = parts[slab, :, lanes:] + parts[following, :, :lanes]
@@ -296,23 +341,31 @@
 
     lax.fori_loop(0, nslab, couple, 0)
 
+    wide = min(2 * width, slots)
+
     def spread(slab, carry):
         below = lax.rem(slab + nslab - 1, nslab)
         value = jnp.concatenate([parts[below, :, lanes:], parts[slab, :, lanes:]], axis=1)
         value = stacked_split(value)
 
         def step(k, inner):
-            both = jnp.dot(value, selector(slab, k), preferred_element_type=jnp.float32)
+            columns = info[slab, 2:3, pl.ds(pl.multiple_of(k * wide, 128), wide)]
+            both = jnp.dot(value, selector(columns, 2 * lanes), preferred_element_type=jnp.float32)
             half = both.shape[0] // 2
             both = both[:half] + both[half:]
-            tiles = [both[c * rows : (c + 1) * rows] for c in range(channel)]
-            for i, tile in enumerate(swap_blocks(tiles, lane_block, width)):
-                proj[slab * groups + k * chunk + i] = tile
+            for q in range(wide // width):
+                tiles = [
+                    both[c * rows : (c + 1) * rows, q * width : (q + 1) * width]
+                    for c in range(channel)
+                ]
+                for i, tile in enumerate(swap_blocks(tiles, lane_block, width)):
+                    proj[slab * groups + k * (wide // GROUP) + q * chunk + i] = tile
             return inner
 
-        lax.fori_loop(0, chunks(slab), step, 0)
+        lax.fori_loop(0, lax.div(table[slab, 1, 0] + (wide - 1), wide), step, 0)
         return carry
 
+    to_scalars.wait()
     lax.fori_loop(0, nslab, spread, 0)
 
     nsum = sums.shape[0]
@@ -386,14 +439,15 @@
 
 
 def apply(arrays, pieces, infos, projections, place, coupling, nslab, slots, rows, ngrid):
-    width = projections[0].shape[2]
+    width = projections[0].shape[0] // rows * GROUP
     lanes = coupling.shape[2]
     depth = arrays[0].shape[1]
     one_sum = ngrid // BOXPTS * rows * 128 * 4
     nsum = 2 if one_sum <= 8 * MIB else 1
     buffers = [
         pltpu.VMEM((nslab * slots // GROUP, rows, width), jnp.float32),
-        pltpu.VMEM((nslab, width // GROUP * rows, 2 * lanes), jnp.float32),
+        pltpu.VMEM((len(pieces) if len(pieces) <= 24 else 1,) + projections[0].shape, jnp.float32),
+        pltpu.VMEM((nslab,) + projections[0].shape, jnp.float32),
         pltpu.VMEM((nslab * slots, depth), jnp.float32),
         pltpu.VMEM((nsum, ngrid // BOXPTS, rows, 128), jnp.float32),
         pltpu.VMEM((2, rows, ngrid // nslab), jnp.float32),
@@ -423,7 +477,7 @@
 Piece = collections.namedtuple("Piece", ["array", "offset", "rows", "info", "index"])
 
 
-def gather_and_project(projectors, described, split, extra, nband, nslab):
+def gather_and_project(projectors, described, mine, split, extra, lanes, nband, nslab):
     slots = projectors.shape[0]
     order, at = cycle_tables(nslab)
     half = slots // 2
@@ -436,9 +490,6 @@
     ]
     backward = [(d, s) for s, d in onward]
     sibling = [(b * nslab + s, (b ^ 1) * nslab + s) for b in range(nband) for s in range(nslab)]
-    core = lax.rem(lax.axis_index("band"), 2)
-    mine = lax.dynamic_slice_in_dim(projectors, core * half, half, 0)
-    mine = jnp.concatenate([described, mine], axis=0)
 
     where = [(0, 0, None)]
     for step in range(1, reach):
@@ -478,7 +529,7 @@
 
     def project_new():
         nonlocal done
-        projections.extend(project(arrays, pieces[done:], place, split))
+        projections.extend(project(arrays, pieces[done:], place, split, lanes))
         done = len(pieces)
 
     project_new()
@@ -520,8 +571,7 @@
     slots = slot_atom.shape[0]
     lanes = round_up(atom_dev, 128)
 
-    slab = lax.axis_index("slab")
-    described = describe(slot_atom, slot_box, slab, nslab, natoms, projectors.shape[1], lanes)
+    described, mine = begin(slot_atom, slot_box, projectors, natoms, lanes)
     mask = (jnp.arange(channel, dtype=jnp.int32)[:, None] < channels[None, :]).astype(jnp.float32)
     masked = coupling * mask[:, None, :] * mask[None, :, :]
     masked = masked.reshape(channel * channel, nslab, atom_dev).transpose(1, 0, 2)
@@ -534,7 +584,7 @@
         x = jnp.pad(x, ((0, padded - rows), (0, 0)))
     split = split_bands(x)
     arrays, pieces, infos, projections, place, masked = gather_and_project(
-        projectors, described, split, masked, nband, nslab
+        projectors, described, mine, split, masked, lanes, nband, nslab
     )
     out = apply(arrays, pieces, infos, projections, place, masked, nslab, slots, padded, ngrid)
     return out[:rows].reshape(nblock, band_local, ngrid)

time: 107 us -> 100 us (0.935); the launches traced: 106 us -> 100 us
  starting transfers between devices: 18.8 us -> 16.7 us
  waiting for transfers between devices: 13.1 us -> 11 us
  other arithmetic: 3.65 us -> 2.33 us
    pallas_call x1, Pallas kernels: 39.2 us -> 32.9 us  [apply(): pl.pallas_call(functools.partial(apply_kernel, nslab, slots, pieces, info...]
    pallas_call x6, Pallas kernels: 21.5 us -> 26.3 us  [project(): pl.pallas_call(functools.partial(project_kernel, local, infos), out_shape...]
    unnamed x8 -> x10, local copies, waits for them, and re-layouts: 0.02 us -> 2.6 us
    ppermute x8, starting transfers between devices: 12.1 us -> 10 us  [gather_and_project(): near = [lax.ppermute(up, AXES, sibling), lax.ppermute(down, AXES, sibling)]]
    ppermute x2, waiting for transfers between devices: 2.03 us -> 4.11 us  [gather_and_project(): down = lax.ppermute(down, AXES, backward)]
    ppermute x2, waiting for transfers between devices: 8.52 us -> 6.52 us  [gather_and_project(): up = lax.ppermute(up, AXES, onward)]
    ppermute x1, waiting for transfers between devices: 1.95 us -> 0.01 us  [gather_and_project(): down = lax.ppermute(down[INFO + quarter:], AXES, backward)]
    reduce_sum x1 -> x0, other arithmetic: 1.36 us -> none  [describe(): jnp.sum((slot_atom >= 0).astype(jnp.int32))]
  transfers between devices with their start and end apart: 16 -> 16, of which waited for: 6 -> 5; matrix products, arithmetic and copies ran while one was open for 3% -> 4% of each run, Pallas kernels for 23% -> 29%
where the time goes in v2:
time: 100 us
  Pallas kernels  65.3 us (65%)
  starting transfers between devices  16.7 us (17%)
  waiting for transfers between devices  11 us (11%)
  local copies, waits for them, and re-layouts  4.55 us (5%)
  other arithmetic  2.33 us (2%)
    pallas_call x1, Pallas kernels, apply(): pl.pallas_call(functools.partial(apply_kernel, nslab, slots, pieces, info...  32.9 us
    pallas_call x6, Pallas kernels, project(): pl.pallas_call(functools.partial(project_kernel, local, infos), out_shape...  26.3 us
    ppermute x8, starting transfers between devices, gather_and_project(): near = [lax.ppermute(up, AXES, sibling), lax.ppermute(down, AXES, sibling)]  10 us
    ppermute x2, waiting for transfers between devices, gather_and_project(): up = lax.ppermute(up, AXES, onward)  6.52 us
    pallas_call x1, Pallas kernels, split_bands(): pl.pallas_call(split_bands_kernel, out_shape=jax.ShapeDtypeStruct(shape,...  5.36 us
    ppermute x2, waiting for transfers between devices, gather_and_project(): down = lax.ppermute(down, AXES, backward)  4.11 us
    unnamed x10, local copies, waits for them, and re-layouts  2.6 us
    ppermute x2, starting transfers between devices, gather_and_project(): up = lax.ppermute(up, AXES, onward)  2.48 us
  transfers between devices with their start and end apart: 16, of which 5 were waited for; matrix products, arithmetic and copies ran while one was open for 4% of the time, Pallas kernels for 29%

profile of v2, /device:TPU:1, one launch (start us, length us, event | category | flops | bytes accessed | tf_op | source)
XLA Modules:
  0.0 100.1 jit_solution(3034525083255844952)
XLA Ops:
  0.0 1.2 %copy-done = f32[512,512]{1,0:T(8,128)S(1)} copy-done((f32[512,512]{1,0:T(8,128)S(1)}, f32[512,512]{1,0:T(8,128)}, u32[]{:S(2)}) %copy-start) | copy-done | bytes 1048600
  2.6 0.8 begin.1
  3.4 2.2 %collective-permute-start = (f32[264,512]{1,0:T(8,128)}, f32[264,512]{1,0:T(8,128)S(1)}, u32[]{:S(2)}, u32[]{:S(2)}) collective-permute-start(f32[264,512]{1,0:T(8,128)} %get-tuple-element.78), channel_id=1, source_target_pairs={{0,2},{2,4},{4,6},{6,7},{7,5},{5,3},{3,1},{1,0},{8,10},{10,12},{12... | collective-permute-start | bytes 1622024 | tf_op jit(solution)/shard_map/ppermute | solution.py:526
  5.6 0.7 constant_dynamic-slice_fusion
  6.4 0.7 fusion
  7.1 1.6 %multiply_multiply_fusion = f32[8,8,768]{2,1,0:T(8,128)} fusion(f32[8,8,768]{2,1,0:T(8,128)} %param.12, f32[8,768]{1,0:T(8,128)S(1)} %fusion), kind=kLoop, calls=%fused_computation.1 | loop fusion | flops 98304 | bytes 417792 | tf_op jit(solution)/shard_map/mul | solution.py:576
  8.7 1.1 %reshape.61 = f32[64,8,96]{2,1,0:T(8,128)S(1)} reshape(f32[8,8,768]{2,1,0:T(8,128)} %multiply_multiply_fusion) | data formatting | bytes 393216 | tf_op jit(solution)/shard_map/reshape | solution.py:577
  9.9 5.4 %split_bands.1.x_ref = bf16[512,16,256]{2,1,0:T(8,128)(2,1)S(1)} custom-call(f32[16,32768]{1,0:T(8,128)S(1)} %bitcast.7), custom_call_target="tpu_custom_call" | custom-call | flops 4194304 | bytes 6291456 | tf_op jit(solution)/shard_map/split_bands/pallas_call | solution.py:63
  15.3 3.0 %project.6.refs_18_ = f32[128,256]{1,0:T(8,128)S(1)} custom-call(s32[51]{0:T(128)S(1)} %reshape.59.place_ref, bf16[512,16,256]{2,1,0:T(8,128)(2,1)S(1)} %split_bands.1.x_ref, f32[8,512]{1,0:T(8,128)S(1)} %get-tuple-element.79.refs_0_, f32[512,512]{1,0:T(8,128)S(1)} %copy-done.1), custom_call_target="tpu_custom_call" | custom-call | flops 134217728 | bytes 5242880 | tf_op jit(solution)/shard_map/project/pallas_call | solution.py:228
  18.6 1.3 %collective-permute-start.2 = (f32[264,512]{1,0:T(8,128)S(1)}, f32[264,512]{1,0:T(8,128)S(1)}, u32[]{:S(2)}, u32[]{:S(2)}) collective-permute-start(f32[264,512]{1,0:T(8,128)S(1)} %collective-permute-done.refs_0_.refs_2_), channel_id=1, source_target_pairs={{0,2},{2,4},{4,6},{6,7},{7,5},{5,3},{3,1},{1,0},{8,10},{10,12},{12... | collective-permute-start | bytes 1622024 | tf_op jit(solution)/shard_map/ppermute | solution.py:551
  20.1 2.4 %collective-permute-start.4 = (f32[264,512]{1,0:T(8,128)S(1)}, f32[264,512]{1,0:T(8,128)S(1)}, u32[]{:S(2)}, u32[]{:S(2)}) collective-permute-start(f32[264,512]{1,0:T(8,128)S(1)} %collective-permute-done.refs_0_.refs_2_), channel_id=1, source_target_pairs={{0,8},{1,9},{2,10},{3,11},{4,12},{5,13},{6,14},{7,15},{8,0},{9,1},... | collective-permute-start | bytes 1622024 | tf_op jit(solution)/shard_map/ppermute | solution.py:549
  22.5 1.7 %project.7 = (f32[128,256]{1,0:T(8,128)S(1)}, f32[128,256]{1,0:T(8,128)S(1)}) custom-call(s32[51]{0:T(128)S(1)} %reshape.59.place_ref, bf16[512,16,256]{2,1,0:T(8,128)(2,1)S(1)} %split_bands.1.x_ref, f32[264,512]{1,0:T(8,128)S(1)} %collective-permute-done.refs_0_.refs_2_, f32[264,512]{1,0:T(8,128)S(1)} %collective-permute-done.1.refs_1_.refs_3_), custom_call_target="tpu_custom_call" | custom-call | flops 134217728 | bytes 5242880 | tf_op jit(solution)/shard_map/project/pallas_call | solution.py:228
  24.2 6.3 %collective-permute-done.2.refs_2_.refs_6_ = f32[264,512]{1,0:T(8,128)S(1)} collective-permute-done((f32[264,512]{1,0:T(8,128)S(1)}, f32[264,512]{1,0:T(8,128)S(1)}, u32[]{:S(2)}, u32[]{:S(2)}) %collective-permute-start.2) | collective-permute-done | bytes 540704 | tf_op jit(solution)/shard_map/ppermute | solution.py:551
  30.5 3.5 %collective-permute-done.3.refs_3_.refs_7_ = f32[264,512]{1,0:T(8,128)S(1)} collective-permute-done((f32[264,512]{1,0:T(8,128)S(1)}, f32[264,512]{1,0:T(8,128)S(1)}, u32[]{:S(2)}, u32[]{:S(2)}) %collective-permute-start.3) | collective-permute-done | bytes 540704 | tf_op jit(solution)/shard_map/ppermute | solution.py:552
  34.0 1.2 %collective-permute-start.6 = (f32[264,512]{1,0:T(8,128)S(1)}, f32[264,512]{1,0:T(8,128)S(1)}, u32[]{:S(2)}, u32[]{:S(2)}) collective-permute-start(f32[264,512]{1,0:T(8,128)S(1)} %collective-permute-done.2.refs_2_.refs_6_), channel_id=1, source_target_pairs={{0,2},{2,4},{4,6},{6,7},{7,5},{5,3},{3,1},{1,0},{8,10},{10,12},{12... | collective-permute-start | bytes 1622024 | tf_op jit(solution)/shard_map/ppermute | solution.py:551
  35.5 2.7 %collective-permute-start.8 = (f32[264,512]{1,0:T(8,128)S(1)}, f32[264,512]{1,0:T(8,128)S(1)}, u32[]{:S(2)}, u32[]{:S(2)}) collective-permute-start(f32[264,512]{1,0:T(8,128)S(1)} %collective-permute-done.2.refs_2_.refs_6_), channel_id=1, source_target_pairs={{0,8},{1,9},{2,10},{3,11},{4,12},{5,13},{6,14},{7,15},{8,0},{9,1},... | collective-permute-start | bytes 1622024 | tf_op jit(solution)/shard_map/ppermute | solution.py:549
  38.2 7.2 %project.8 = (f32[128,256]{1,0:T(8,128)S(1)}, f32[128,256]{1,0:T(8,128)S(1)}, f32[128,256]{1,0:T(8,128)S(1)}, f32[128,256]{1,0:T(8,128)S(1)}) custom-call(s32[51]{0:T(128)S(1)} %reshape.59.place_ref, bf16[512,16,256]{2,1,0:T(8,128)(2,1)S(1)} %split_bands.1.x_ref, f32[264,512]{1,0:T(8,128)S(1)} %collective-permute-done.4.refs_0_.refs_4_, ...), custom_call_target="tpu_custom_call" | custom-call | flops 268435456 | bytes 6291456 | tf_op jit(solution)/shard_map/project/pallas_call | solution.py:228
  46.3 3.6 %collective-permute-start.12 = (f32[264,512]{1,0:T(8,128)S(1)}, f32[264,512]{1,0:T(8,128)S(1)}, u32[]{:S(2)}, u32[]{:S(2)}) collective-permute-start(f32[264,512]{1,0:T(8,128)S(1)} %collective-permute-done.6.refs_2_.refs_10_), channel_id=1, source_target_pairs={{0,8},{1,9},{2,10},{3,11},{4,12},{5,13},{6,14},{7,15},{8,0},{9,1},... | collective-permute-start | bytes 1622024 | tf_op jit(solution)/shard_map/ppermute | solution.py:549
  50.0 1.0 collective-permute-start.10
  51.6 7.6 %project.9 = (f32[128,256]{1,0:T(8,128)S(1)}, f32[128,256]{1,0:T(8,128)S(1)}, f32[128,256]{1,0:T(8,128)S(1)}, f32[128,256]{1,0:T(8,128)S(1)}) custom-call(s32[51]{0:T(128)S(1)} %reshape.59.place_ref, bf16[512,16,256]{2,1,0:T(8,128)(2,1)S(1)} %split_bands.1.x_ref, f32[264,512]{1,0:T(8,128)S(1)} %collective-permute-done.8.refs_0_.refs_8_, ...), custom_call_target="tpu_custom_call" | custom-call | flops 268435456 | bytes 6291456 | tf_op jit(solution)/shard_map/project/pallas_call | solution.py:228
  59.2 1.1 %collective-permute-start.14 = (f32[136,512]{1,0:T(8,128)S(1)}, f32[136,512]{1,0:T(8,128)S(1)}, u32[]{:S(2)}, u32[]{:S(2)}) collective-permute-start(f32[136,512]{1,0:T(8,128)S(1)} %collective-permute-done.10.refs_2_.refs_14_), channel_id=1, source_target_pairs={{0,8},{1,9},{2,10},{3,11},{4,12},{5,13},{6,14},{7,15},{8,0},{9,1},... | collective-permute-start | bytes 835592 | tf_op jit(solution)/shard_map/ppermute | solution.py:549
  60.4 4.7 %project.10 = (f32[128,256]{1,0:T(8,128)S(1)}, f32[128,256]{1,0:T(8,128)S(1)}, f32[128,256]{1,0:T(8,128)S(1)}, f32[128,256]{1,0:T(8,128)S(1)}) custom-call(s32[51]{0:T(128)S(1)} %reshape.59.place_ref, bf16[512,16,256]{2,1,0:T(8,128)(2,1)S(1)} %split_bands.1.x_ref, f32[264,512]{1,0:T(8,128)S(1)} %collective-permute-done.12.refs_0_.refs_12_, ...), custom_call_target="tpu_custom_call" | custom-call | flops 201326592 | bytes 5767168 | tf_op jit(solution)/shard_map/project/pallas_call | solution.py:228
  65.1 2.2 %project.11 = (f32[128,256]{1,0:T(8,128)S(1)}, f32[128,256]{1,0:T(8,128)S(1)}) custom-call(s32[51]{0:T(128)S(1)} %reshape.59.place_ref, bf16[512,16,256]{2,1,0:T(8,128)(2,1)S(1)} %split_bands.1.x_ref, f32[136,512]{1,0:T(8,128)S(1)} %collective-permute-done.14.refs_0_.refs_16_, f32[128,512]{1,0:T(8,128)S(1)} %collective-permute-done.15.refs_1_.refs_17_), custom_call_target="tpu_custom_call" | custom-call | flops 67108864 | bytes 4718592 | tf_op jit(solution)/shard_map/project/pallas_call | solution.py:228
  67.2 32.9 %apply.1 = f32[16,32768]{1,0:T(8,128)} custom-call(s32[51]{0:T(128)S(1)} %reshape.59.place_ref, f32[8,64,128]{2,1,0:T(8,128)S(1)} %pad.4.coupling_ref, f32[8,512]{1,0:T(8,128)S(1)} %get-tuple-element.79.refs_0_, f32[512,512]{1,0:T(8,128)S(1)} %copy-done.1, f32[264,512]{1,0:T(8,128)S(1)} %collective-permute-done.refs_0_.refs_2_, ...), custom_call_target="tpu_custom_call" | custom-call | tf_op jit(solution)/shard_map/apply/pallas_call | solution.py:466
  (36 shorter events, 4.0 us)
Async XLA Ops:
  0.0 1.2 %copy-start = (f32[512,512]{1,0:T(8,128)S(1)}, f32[512,512]{1,0:T(8,128)}, u32[]{:S(2)}) copy-start(f32[512,512]{1,0:T(8,128)} %refs_1_.3) | copy-start | bytes 3145732
  1.2 0.7 copy-start.3
  1.9 0.7 copy-start.4
  2.6 7.3 %copy-start.2 = (f32[2,8,32768]{2,1,0:T(8,128)S(1)}, f32[2,8,32768]{2,1,0:T(8,128)}, u32[]{:S(2)}) copy-start(f32[2,8,32768]{2,1,0:T(8,128)} %param.7) | copy-start | bytes 6291460
  3.4 14.8 %collective-permute-start = (f32[264,512]{1,0:T(8,128)}, f32[264,512]{1,0:T(8,128)S(1)}, u32[]{:S(2)}, u32[]{:S(2)}) collective-permute-start(f32[264,512]{1,0:T(8,128)} %get-tuple-element.78), channel_id=1, source_target_pairs={{0,2},{2,4},{4,6},{6,7},{7,5},{5,3},{3,1},{1,0},{8,10},{10,12},{12... | collective-permute-start | bytes 1622024 | tf_op jit(solution)/shard_map/ppermute | solution.py:526
  5.6 13.0 %collective-permute-start.1 = (f32[264,512]{1,0:T(8,128)}, f32[264,512]{1,0:T(8,128)S(1)}, u32[]{:S(2)}, u32[]{:S(2)}) collective-permute-start(f32[264,512]{1,0:T(8,128)} %get-tuple-element.78), channel_id=1, source_target_pairs={{2,0},{4,2},{6,4},{7,6},{5,7},{3,5},{1,3},{0,1},{10,8},{12,10},{14... | collective-permute-start | bytes 1622024 | tf_op jit(solution)/shard_map/ppermute | solution.py:527
  9.9 5.4 %copy-start.1 = (f32[512,512]{1,0:T(8,128)S(1)}, f32[512,512]{1,0:T(8,128)}, u32[]{:S(2)}) copy-start(f32[512,512]{1,0:T(8,128)} %refs_1_.3) | copy-start | bytes 3145732
  18.6 11.9 %collective-permute-start.2 = (f32[264,512]{1,0:T(8,128)S(1)}, f32[264,512]{1,0:T(8,128)S(1)}, u32[]{:S(2)}, u32[]{:S(2)}) collective-permute-start(f32[264,512]{1,0:T(8,128)S(1)} %collective-permute-done.refs_0_.refs_2_), channel_id=1, source_target_pairs={{0,2},{2,4},{4,6},{6,7},{7,5},{5,3},{3,1},{1,0},{8,10},{10,12},{12... | collective-permute-start | bytes 1622024 | tf_op jit(solution)/shard_map/ppermute | solution.py:551
  19.9 14.1 %collective-permute-start.3 = (f32[264,512]{1,0:T(8,128)S(1)}, f32[264,512]{1,0:T(8,128)S(1)}, u32[]{:S(2)}, u32[]{:S(2)}) collective-permute-start(f32[264,512]{1,0:T(8,128)S(1)} %collective-permute-done.1.refs_1_.refs_3_), channel_id=1, source_target_pairs={{2,0},{4,2},{6,4},{7,6},{5,7},{3,5},{1,3},{0,1},{10,8},{12,10},{14... | collective-permute-start | bytes 1622024 | tf_op jit(solution)/shard_map/ppermute | solution.py:552
  20.1 13.9 %collective-permute-start.4 = (f32[264,512]{1,0:T(8,128)S(1)}, f32[264,512]{1,0:T(8,128)S(1)}, u32[]{:S(2)}, u32[]{:S(2)}) collective-permute-start(f32[264,512]{1,0:T(8,128)S(1)} %collective-permute-done.refs_0_.refs_2_), channel_id=1, source_target_pairs={{0,8},{1,9},{2,10},{3,11},{4,12},{5,13},{6,14},{7,15},{8,0},{9,1},... | collective-permute-start | bytes 1622024 | tf_op jit(solution)/shard_map/ppermute | solution.py:549
  22.5 11.5 %collective-permute-start.5 = (f32[264,512]{1,0:T(8,128)S(1)}, f32[264,512]{1,0:T(8,128)S(1)}, u32[]{:S(2)}, u32[]{:S(2)}) collective-permute-start(f32[264,512]{1,0:T(8,128)S(1)} %collective-permute-done.1.refs_1_.refs_3_), channel_id=1, source_target_pairs={{0,8},{1,9},{2,10},{3,11},{4,12},{5,13},{6,14},{7,15},{8,0},{9,1},... | collective-permute-start | bytes 1622024 | tf_op jit(solution)/shard_map/ppermute | solution.py:549
  34.0 11.6 %collective-permute-start.6 = (f32[264,512]{1,0:T(8,128)S(1)}, f32[264,512]{1,0:T(8,128)S(1)}, u32[]{:S(2)}, u32[]{:S(2)}) collective-permute-start(f32[264,512]{1,0:T(8,128)S(1)} %collective-permute-done.2.refs_2_.refs_6_), channel_id=1, source_target_pairs={{0,2},{2,4},{4,6},{6,7},{7,5},{5,3},{3,1},{1,0},{8,10},{10,12},{12... | collective-permute-start | bytes 1622024 | tf_op jit(solution)/shard_map/ppermute | solution.py:551
  35.2 11.0 %collective-permute-start.7 = (f32[264,512]{1,0:T(8,128)S(1)}, f32[264,512]{1,0:T(8,128)S(1)}, u32[]{:S(2)}, u32[]{:S(2)}) collective-permute-start(f32[264,512]{1,0:T(8,128)S(1)} %collective-permute-done.3.refs_3_.refs_7_), channel_id=1, source_target_pairs={{2,0},{4,2},{6,4},{7,6},{5,7},{3,5},{1,3},{0,1},{10,8},{12,10},{14... | collective-permute-start | bytes 1622024 | tf_op jit(solution)/shard_map/ppermute | solution.py:552
  35.5 10.8 %collective-permute-start.8 = (f32[264,512]{1,0:T(8,128)S(1)}, f32[264,512]{1,0:T(8,128)S(1)}, u32[]{:S(2)}, u32[]{:S(2)}) collective-permute-start(f32[264,512]{1,0:T(8,128)S(1)} %collective-permute-done.2.refs_2_.refs_6_), channel_id=1, source_target_pairs={{0,8},{1,9},{2,10},{3,11},{4,12},{5,13},{6,14},{7,15},{8,0},{9,1},... | collective-permute-start | bytes 1622024 | tf_op jit(solution)/shard_map/ppermute | solution.py:549
  38.2 8.0 %collective-permute-start.9 = (f32[264,512]{1,0:T(8,128)S(1)}, f32[264,512]{1,0:T(8,128)S(1)}, u32[]{:S(2)}, u32[]{:S(2)}) collective-permute-start(f32[264,512]{1,0:T(8,128)S(1)} %collective-permute-done.3.refs_3_.refs_7_), channel_id=1, source_target_pairs={{0,8},{1,9},{2,10},{3,11},{4,12},{5,13},{6,14},{7,15},{8,0},{9,1},... | collective-permute-start | bytes 1622024 | tf_op jit(solution)/shard_map/ppermute | solution.py:549
  46.3 12.9 %collective-permute-start.12 = (f32[264,512]{1,0:T(8,128)S(1)}, f32[264,512]{1,0:T(8,128)S(1)}, u32[]{:S(2)}, u32[]{:S(2)}) collective-permute-start(f32[264,512]{1,0:T(8,128)S(1)} %collective-permute-done.6.refs_2_.refs_10_), channel_id=1, source_target_pairs={{0,8},{1,9},{2,10},{3,11},{4,12},{5,13},{6,14},{7,15},{8,0},{9,1},... | collective-permute-start | bytes 1622024 | tf_op jit(solution)/shard_map/ppermute | solution.py:549
  49.9 9.3 %collective-permute-start.13 = (f32[264,512]{1,0:T(8,128)S(1)}, f32[264,512]{1,0:T(8,128)S(1)}, u32[]{:S(2)}, u32[]{:S(2)}) collective-permute-start(f32[264,512]{1,0:T(8,128)S(1)} %collective-permute-done.7.refs_3_.refs_11_), channel_id=1, source_target_pairs={{0,8},{1,9},{2,10},{3,11},{4,12},{5,13},{6,14},{7,15},{8,0},{9,1},... | collective-permute-start | bytes 1622024 | tf_op jit(solution)/shard_map/ppermute | solution.py:549
  50.0 9.2 %collective-permute-start.10 = (f32[136,512]{1,0:T(8,128)S(1)}, f32[136,512]{1,0:T(8,128)S(1)}, u32[]{:S(2)}, u32[]{:S(2)}) collective-permute-start(f32[136,512]{1,0:T(8,128)S(1)} %slice.6), channel_id=1, source_target_pairs={{0,2},{2,4},{4,6},{6,7},{7,5},{5,3},{3,1},{1,0},{8,10},{10,12},{12... | collective-permute-start | bytes 835592 | tf_op jit(solution)/shard_map/ppermute | solution.py:554
  51.0 8.2 %collective-permute-start.11 = (f32[128,512]{1,0:T(8,128)S(1)}, f32[128,512]{1,0:T(8,128)S(1)}, u32[]{:S(2)}, u32[]{:S(2)}) collective-permute-start(f32[128,512]{1,0:T(8,128)S(1)} %slice.7), channel_id=1, source_target_pairs={{2,0},{4,2},{6,4},{7,6},{5,7},{3,5},{1,3},{0,1},{10,8},{12,10},{14... | collective-permute-start | bytes 786440 | tf_op jit(solution)/shard_map/ppermute | solution.py:555
  59.2 5.8 %collective-permute-start.14 = (f32[136,512]{1,0:T(8,128)S(1)}, f32[136,512]{1,0:T(8,128)S(1)}, u32[]{:S(2)}, u32[]{:S(2)}) collective-permute-start(f32[136,512]{1,0:T(8,128)S(1)} %collective-permute-done.10.refs_2_.refs_14_), channel_id=1, source_target_pairs={{0,8},{1,9},{2,10},{3,11},{4,12},{5,13},{6,14},{7,15},{8,0},{9,1},... | collective-permute-start | bytes 835592 | tf_op jit(solution)/shard_map/ppermute | solution.py:549
  60.3 4.8 %collective-permute-start.15 = (f32[128,512]{1,0:T(8,128)S(1)}, f32[128,512]{1,0:T(8,128)S(1)}, u32[]{:S(2)}, u32[]{:S(2)}) collective-permute-start(f32[128,512]{1,0:T(8,128)S(1)} %collective-permute-done.11.refs_3_.refs_15_), channel_id=1, source_target_pairs={{0,8},{1,9},{2,10},{3,11},{4,12},{5,13},{6,14},{7,15},{8,0},{9,1},... | collective-permute-start | bytes 786440 | tf_op jit(solution)/shard_map/ppermute | solution.py:549
